TPU v7x, 128 devices: a whole 4x4x4 slice. The times are simulated.
128 devices in a mesh: slab: 8 (over z, core), tile: 16 (over y, x).
Axes of the slice: x: 4, y: 4, z: 4, core: 2. Of those that a mesh axis runs over, the one named last changes fastest.
Arguments:
- adjoint: float32 [128, 1024, 1024], P('slab', 'tile'), may hold values from -6 to 6
- adjoint_prev: float32 [128, 1024, 1024], P('slab', 'tile'), may hold values from -6 to 6
- courant: float32 [128, 1024, 1024], P('slab', 'tile'), may hold values from 0.15 to 0.5
- wall_cell: int32 [262144], P(('slab', 'tile')), may hold values from 0 to 1048575
- wall_patch: int32 [262144], P(('slab', 'tile')), may hold values from 0 to 4095, as said below
- block_count: int32 [2048], P(('slab', 'tile')), may hold values from 1 to 128, as said below
- wall_damp: float32 [262144], P(('slab', 'tile')), may hold values from 0.1 to 0.6
- history: bfloat16 [3, 262144, 256], P(None, ('slab', 'tile')), may hold values from -1.1953125 to 1.1953125
Outputs:
- patch_gradient: float32 [4096, 256], P('tile')
- final_adjoint: float32 [128, 1024, 1024], P('slab', 'tile')
- previous_adjoint: float32 [128, 1024, 1024], P('slab', 'tile')
Inputs may be any that keep to these rules, and one draw needn't show every extreme that they name: `wall_patch`: A slot in block j (slots j * 128 to (j + 1) * 128 - 1 of its device) names a patch from j * (256) to (j + 1) * 256 - 1, whether live or not. `block_count`: in every draw one owner tile gets 128 live slots from every device.
All inputs are finite; a program needn't handle non-finite values.
Results may differ from a plain program's by a relative error of at most 0.0029.
Values may be sent and summed in bfloat16 or wider, within the bound.
A program may use at most 128 MiB of HBM per device.

v0:
```python
import jax
import jax.numpy as jnp
from jax import lax
from jax.sharding import PartitionSpec as P

PATCHES = 4096


face_weight = 0.5
edge_weight = 0.125
corner_weight = 0.0625


def extended(cells, sides, width):
    for axis, dim in sides:
        count = lax.axis_size(axis)
        ends = count - 1
        head = lax.slice_in_dim(cells, 0, width, axis=dim)
        tail = lax.slice_in_dim(cells, cells.shape[dim] - width, cells.shape[dim], axis=dim)
        cells = jnp.concatenate(
            [
                lax.ppermute(tail, axis, [(i, (i + 1) % count) for i in range(ends)]),
                cells,
                lax.ppermute(head, axis, [((i + 1) % count, i) for i in range(ends)]),
            ],
            axis=dim,
        )
    return cells


def x_sides(field):
    zero_col = jnp.zeros(field.shape[:-1] + (1,), field.dtype)
    from_left = jnp.concatenate([zero_col, field[:, :, :-1]], axis=2)
    from_right = jnp.concatenate([field[:, :, 1:], zero_col], axis=2)
    return from_left + from_right


def stencil(padded):
    side_x = x_sides(padded)
    mid_mid = padded[:, 1:-1]
    mid_side = padded[:, :-2] + padded[:, 2:]
    side_mid = side_x[:, 1:-1]
    side_side = side_x[:, :-2] + side_x[:, 2:]
    center = mid_mid[1:-1]
    face_z = mid_mid[:-2] + mid_mid[2:]
    faces = face_z + mid_side[1:-1] + side_mid[1:-1]
    edges = mid_side[:-2] + mid_side[2:] + (side_mid[:-2] + side_mid[2:]) + side_side[1:-1]
    corners = side_side[:-2] + side_side[2:]
    return face_weight * faces + edge_weight * edges + corner_weight * corners - 5.0 * center


def extend(field):
    padded = extended(field, (("slab", 0), ("tile", 1)), 1)
    return padded


def on_device(
    adjoint, adjoint_prev, courant, wall_cell, wall_patch, block_count, wall_damp, history
):
    tiles = lax.axis_size("tile")
    steps, slots, width = history.shape
    cap = slots // tiles
    per_owner = PATCHES // tiles
    depth, height, across = adjoint.shape
    limit = jnp.broadcast_to(block_count[:, None], (tiles, cap)).reshape(-1)
    live = (jnp.arange(slots, dtype=jnp.int32) % cap < limit).astype(jnp.float32)
    coeff = wall_damp * live
    cell_z = wall_cell // (height * across)
    cell_y = wall_cell // across % height
    cell_x = wall_cell % across
    lam = adjoint
    prev = adjoint_prev
    acc = jnp.zeros((slots, width), jnp.float32)
    for step in range(steps):
        laplace = stencil(extend(lam))
        following = 2.0 * lam - prev + courant * laplace
        change = -coeff * (lam[cell_z, cell_y, cell_x] - prev[cell_z, cell_y, cell_x])
        updated = following.at[cell_z, cell_y, cell_x].add(change)
        acc = acc + updated[cell_z, cell_y, cell_x][:, None] * history[step].astype(jnp.float32)
        prev = lam
        lam = updated
    wall_rows = (acc * live[:, None]).astype(jnp.bfloat16)
    owned = jnp.where(live > 0.0, wall_patch, -1)
    row_blocks = wall_rows.reshape(tiles, cap, width)
    id_blocks = owned.reshape(tiles, cap)
    got_rows, got_ids = (
        lax.all_to_all(row_blocks, "tile", split_axis=0, concat_axis=0, tiled=True),
        lax.all_to_all(id_blocks, "tile", split_axis=0, concat_axis=0, tiled=True),
    )
    local = got_ids.reshape(-1) - lax.axis_index("tile") * per_owner
    onehot = (local[None, :] == jnp.arange(per_owner, dtype=jnp.int32)[:, None]).astype(
        jnp.bfloat16
    )
    partial_sum = jnp.dot(onehot, got_rows.reshape(-1, width), preferred_element_type=jnp.float32)
    gradient = lax.psum(partial_sum, "slab")
    return (gradient, lam, prev)


def solution(mesh):
    return jax.shard_map(
        on_device,
        mesh=mesh,
        in_specs=(
            P("slab", "tile", None),
            P("slab", "tile", None),
            P("slab", "tile", None),
            P(("slab", "tile")),
            P(("slab", "tile")),
            P(("slab", "tile")),
            P(("slab", "tile")),
            P(None, ("slab", "tile"), None),
        ),
        out_specs=(P("tile", None), P("slab", "tile", None), P("slab", "tile", None)),
        check_vma=False,
    )
```

profile of v0, /device:TPU:1, one launch (start us, length us, event | category | flops | bytes accessed | tf_op | source)
XLA Modules:
  0.0 505.7 jit_solution(10774859932733882507)
XLA Ops:
  8.2 4.9 collective-permute-start
  13.2 1.9 collective-permute-start.1
  17.4 28.8 %gather_fusion = f32[2048]{0:T(1024)S(1)} fusion(f32[16,64,1024]{2,1,0:T(8,128)} %param.8, s32[2048]{0:T(1024)S(1)} %bitcast.35), kind=kCustom, calls=%fused_computation | custom fusion | bytes 40960 | tf_op jit(solution)/shard_map/gather | solution.py:77
  46.2 28.8 %gather_fusion.1 = f32[2048]{0:T(1024)S(1)} fusion(f32[16,64,1024]{2,1,0:T(8,128)} %param.9, s32[2048]{0:T(1024)S(1)} %bitcast.36), kind=kCustom, calls=%fused_computation.1 | custom fusion | bytes 40960 | tf_op jit(solution)/shard_map/gather | solution.py:77
  75.2 2.8 constant_dynamic-update-slice_fusion.1
  78.1 3.1 collective-permute-start.2
  83.0 3.7 collective-permute-done.3
  88.4 6.0 %fusion.76 = (f32[18,66,1023]{2,1,0:T(8,128)}, f32[18,66,1023]{2,1,0:T(8,128)}) fusion(f32[18,66,1024]{2,1,0:T(8,128)S(1)} %pad_maximum_fusion), kind=kLoop, calls=%fused_computation.172 | loop fusion | bytes 19445184 | tf_op jit(solution)/shard_map/slice | solution.py:34
  94.4 8.3 %fusion.4 = f32[18,64,1024]{2,1,0:T(8,128)S(1)} fusion(f32[18,66,1023]{2,1,0:T(8,128)} %get-tuple-element.7, f32[18,66,1023]{2,1,0:T(8,128)} %get-tuple-element.8), kind=kLoop, calls=%fused_computation.22 | loop fusion | flops 3538944 | bytes 14441184 | tf_op jit(solution)/shard_map/add | solution.py:43
  102.6 16.6 %fusion.13 = f32[16,64,1024]{2,1,0:T(8,128)} fusion(f32[16,64,1024]{2,1,0:T(8,128)} %param.10, f32[18,66,1023]{2,1,0:T(8,128)} %get-tuple-element.8, f32[18,66,1023]{2,1,0:T(8,128)} %get-tuple-element.7, f32[18,64,1024]{2,1,0:T(8,128)S(1)} %fusion.4, f32[18,64,1024]{2,1,0:T(8,128)S(1)} %fusion.5, f32[1,64,1024]{2,1,0:T(8,128)S(1)} %collective-permute-done.1, ...), kind=kLoop, calls=%fused_computation.51 | loop fusion | flops 25165824 | bytes 52189920 | tf_op jit(solution)/shard_map/add | solution.py:76
  119.2 5.2 %copy.29 = f32[128,8,8,128]{3,1,2,0:T(8,128)} copy(f32[128,8,8,128]{3,2,1,0:T(8,128)} %bitcast.44) | data formatting | bytes 8388608
  124.4 14.5 %scatter_fusion = f32[1048576]{0:T(1024)} fusion(f32[1048576]{0:T(1024)} %bitcast.40, s32[2048]{0:T(1024)S(1)} %broadcast_select_fusion, f32[2048]{0:T(1024)S(1)} %subtract_multiply_fusion.2), kind=kCustom, calls=%fused_computation.5 | custom fusion | flops 2048 | bytes 32768
  140.0 5.2 %collective-permute-start.4 = (f32[1,64,1024]{2,1,0:T(8,128)S(1)}, f32[1,64,1024]{2,1,0:T(8,128)S(1)}, u32[]{:S(2)}, u32[]{:S(2)}) collective-permute-start(f32[1,64,1024]{2,1,0:T(8,128)S(1)} %reshape.87), channel_id=1, source_target_pairs={{0,16},{16,32},{32,48},{48,64},{64,80},{80,96},{96,112},{1,17},{17... | collective-permute-start | bytes 786440 | tf_op jit(solution)/shard_map/ppermute | solution.py:22
  145.9 8.3 %all-to-all-start = ((s32[16,1,128]{2,1,0:T(1,128)}), s32[16,1,128]{2,1,0:T(1,128)S(1)}, u32[]{:S(2)}, u32[]{:S(2)}) async-start(s32[16,1,128]{2,1,0:T(1,128)} %bitcast.1), calls=%async_computation | async-start | bytes 16384 | tf_op jit(solution)/shard_map/all_to_all | solution.py:88
  154.2 4.9 reshape.78
  159.2 1.9 collective-permute-start.5
  161.1 28.8 %gather_fusion.2 = f32[2048]{0:T(1024)S(1)} fusion(f32[16,64,1024]{2,1,0:T(8,128)} %reshape.78, s32[2048]{0:T(1024)S(1)} %bitcast.37), kind=kCustom, calls=%fused_computation.2 | custom fusion | bytes 40960 | tf_op jit(solution)/shard_map/gather | solution.py:79
  189.9 2.8 constant_dynamic-update-slice_fusion.4
  192.9 3.3 collective-permute-start.6
  196.2 1.5 collective-permute-start.7
  197.9 3.7 collective-permute-done.7
  203.3 5.8 %fusion.75 = (f32[18,66,1023]{2,1,0:T(8,128)}, f32[18,66,1023]{2,1,0:T(8,128)}) fusion(f32[18,66,1024]{2,1,0:T(8,128)S(1)} %pad_maximum_fusion.1), kind=kLoop, calls=%fused_computation.171 | loop fusion | bytes 19445184 | tf_op jit(solution)/shard_map/slice | solution.py:34
  209.1 10.5 %fusion.2 = f32[18,64,1024]{2,1,0:T(8,128)} fusion(f32[18,66,1023]{2,1,0:T(8,128)} %get-tuple-element.5, f32[18,66,1023]{2,1,0:T(8,128)} %get-tuple-element.6), kind=kLoop, calls=%fused_computation.17 | loop fusion | flops 3538944 | bytes 14441184 | tf_op jit(solution)/shard_map/add | solution.py:43
  219.6 19.0 %fusion.27 = f32[16,64,1024]{2,1,0:T(8,128)} fusion(f32[16,64,1024]{2,1,0:T(8,128)} %param.10, f32[18,66,1023]{2,1,0:T(8,128)} %get-tuple-element.6, f32[18,66,1023]{2,1,0:T(8,128)} %get-tuple-element.5, f32[18,64,1024]{2,1,0:T(8,128)} %fusion.2, f32[18,64,1024]{2,1,0:T(8,128)S(1)} %fusion.3, f32[1,64,1024]{2,1,0:T(8,128)S(1)} %collective-permute-done.5, ...), kind=kLoop, calls=%fused_computation.65 | loop fusion | flops 25165824 | bytes 52189920 | tf_op jit(solution)/shard_map/add | solution.py:76
  238.6 5.1 %copy.30 = f32[128,8,8,128]{3,1,2,0:T(8,128)} copy(f32[128,8,8,128]{3,2,1,0:T(8,128)} %bitcast.45) | data formatting | bytes 8388608
  243.7 14.4 %scatter_fusion.1 = f32[1048576]{0:T(1024)} fusion(f32[1048576]{0:T(1024)} %bitcast.41, s32[2048]{0:T(1024)S(1)} %broadcast_select_fusion, f32[2048]{0:T(1024)S(1)} %subtract_multiply_fusion.1), kind=kCustom, calls=%fused_computation.6 | custom fusion | flops 2048 | bytes 32768
  259.3 5.1 %collective-permute-start.8 = (f32[1,64,1024]{2,1,0:T(8,128)S(1)}, f32[1,64,1024]{2,1,0:T(8,128)S(1)}, u32[]{:S(2)}, u32[]{:S(2)}) collective-permute-start(f32[1,64,1024]{2,1,0:T(8,128)S(1)} %reshape.89), channel_id=1, source_target_pairs={{0,16},{16,32},{32,48},{48,64},{64,80},{80,96},{96,112},{1,17},{17... | collective-permute-start | bytes 786440 | tf_op jit(solution)/shard_map/ppermute | solution.py:22
  264.4 3.1 fusion.83
  267.5 4.9 reshape.82
  272.4 28.8 %gather_fusion.3 = f32[2048]{0:T(1024)S(1)} fusion(f32[16,64,1024]{2,1,0:T(8,128)} %reshape.82, s32[2048]{0:T(1024)S(1)} %bitcast.38), kind=kCustom, calls=%fused_computation.3 | custom fusion | bytes 40960 | tf_op jit(solution)/shard_map/gather | solution.py:79
  302.0 1.9 collective-permute-start.9
  303.9 2.8 constant_dynamic-update-slice_fusion.7
  306.7 3.2 collective-permute-done.9
  310.0 3.1 collective-permute-start.10
  313.1 1.5 collective-permute-start.11
  314.8 3.6 collective-permute-done.11
  320.2 5.8 %fusion.74 = (f32[18,66,1023]{2,1,0:T(8,128)}, f32[18,66,1023]{2,1,0:T(8,128)}) fusion(f32[18,66,1024]{2,1,0:T(8,128)S(1)} %pad_maximum_fusion.2), kind=kLoop, calls=%fused_computation.170 | loop fusion | bytes 19445184 | tf_op jit(solution)/shard_map/slice | solution.py:34
  326.0 10.5 %fusion = f32[18,64,1024]{2,1,0:T(8,128)} fusion(f32[18,66,1023]{2,1,0:T(8,128)} %get-tuple-element.3, f32[18,66,1023]{2,1,0:T(8,128)} %get-tuple-element.4), kind=kLoop, calls=%fused_computation.12 | loop fusion | flops 3538944 | bytes 14441184 | tf_op jit(solution)/shard_map/add | solution.py:43
  336.5 19.0 %fusion.41 = f32[16,64,1024]{2,1,0:T(8,128)} fusion(f32[16,64,1024]{2,1,0:T(8,128)} %param.10, f32[18,66,1023]{2,1,0:T(8,128)} %get-tuple-element.4, f32[18,66,1023]{2,1,0:T(8,128)} %get-tuple-element.3, f32[18,64,1024]{2,1,0:T(8,128)} %fusion, f32[18,64,1024]{2,1,0:T(8,128)S(1)} %fusion.1, f32[1,64,1024]{2,1,0:T(8,128)S(1)} %collective-permute-done.9, ...), kind=kLoop, calls=%fused_computation.79 | loop fusion | flops 25165824 | bytes 52189920 | tf_op jit(solution)/shard_map/add | solution.py:76
  355.5 5.1 %copy.31 = f32[128,8,8,128]{3,1,2,0:T(8,128)} copy(f32[128,8,8,128]{3,2,1,0:T(8,128)} %bitcast.43) | data formatting | bytes 8388608
  360.7 14.4 %scatter_fusion.2 = f32[1048576]{0:T(1024)} fusion(f32[1048576]{0:T(1024)} %bitcast.42, s32[2048]{0:T(1024)S(1)} %broadcast_select_fusion, f32[2048]{0:T(1024)S(1)} %subtract_multiply_fusion), kind=kCustom, calls=%fused_computation.7 | custom fusion | flops 2048 | bytes 32768
  375.1 4.9 reshape.86
  380.0 28.8 %gather_fusion.4 = f32[2048]{0:T(1024)S(1)} fusion(f32[16,64,1024]{2,1,0:T(8,128)} %reshape.86, s32[2048]{0:T(1024)S(1)} %bitcast.39), kind=kCustom, calls=%fused_computation.4 | custom fusion | bytes 40960 | tf_op jit(solution)/shard_map/gather | solution.py:79
  408.8 3.1 fusion.56
  411.9 8.9 %all-to-all-start.1 = ((bf16[16,128,256]{2,1,0:T(8,128)(2,1)}), bf16[16,128,256]{2,1,0:T(8,128)(2,1)S(1)}, u32[]{:S(2)}, u32[]{:S(2)}) async-start(bf16[16,128,256]{2,1,0:T(8,128)(2,1)} %fusion.56), calls=%async_computation.1 | async-start | bytes 2097152 | tf_op jit(solution)/shard_map/all_to_all | solution.py:87
  420.9 15.2 %all-to-all-done.1 = bf16[16,128,256]{2,1,0:T(8,128)(2,1)S(1)} async-done(((bf16[16,128,256]{2,1,0:T(8,128)(2,1)}), bf16[16,128,256]{2,1,0:T(8,128)(2,1)S(1)}, u32[]{:S(2)}, u32[]{:S(2)}) %all-to-all-start.1) | async-done | bytes 1048608 | tf_op jit(solution)/shard_map/all_to_all | solution.py:87
  437.3 59.4 %all-reduce.8.cloned.1.call-done = f32[256,256]{1,0:T(8,128)} async-done(((f32[256,256]{1,0:T(8,128)}), f32[256,256]{1,0:T(8,128)}) %all-reduce.8.cloned.1.call-update) | async-done | bytes 262160 | tf_op jit(solution)/shard_map/psum | solution.py:95
  496.7 1.7 copy.42
  (74 shorter events, 16.0 us)
Async XLA Ops:
  8.2 66.9 %collective-permute-start = (f32[1,64,1024]{2,1,0:T(8,128)S(1)}, f32[1,64,1024]{2,1,0:T(8,128)S(1)}, u32[]{:S(2)}, u32[]{:S(2)}) collective-permute-start(f32[1,64,1024]{2,1,0:T(8,128)S(1)} %get-tuple-element.20), channel_id=1, source_target_pairs={{0,16},{16,32},{32,48},{48,64},{64,80},{80,96},{96,112},{1,17},{17... | collective-permute-start | bytes 786440 | tf_op jit(solution)/shard_map/ppermute | solution.py:22
  13.2 64.8 %collective-permute-start.1 = (f32[1,64,1024]{2,1,0:T(8,128)S(1)}, f32[1,64,1024]{2,1,0:T(8,128)S(1)}, u32[]{:S(2)}, u32[]{:S(2)}) collective-permute-start(f32[1,64,1024]{2,1,0:T(8,128)S(1)} %get-tuple-element.19), channel_id=1, source_target_pairs={{16,0},{32,16},{48,32},{64,48},{80,64},{96,80},{112,96},{17,1},{33... | collective-permute-start | bytes 786440 | tf_op jit(solution)/shard_map/ppermute | solution.py:24
  46.2 28.8 %copy-start.5 = (f32[2048]{0:T(1024)S(1)}, f32[2048]{0:T(1024)}, u32[]{:S(2)}) copy-start(f32[2048]{0:T(1024)} %param.14) | copy-start | bytes 24580
  46.2 28.8 %copy-start.6 = (s32[16]{0:T(128)S(1)}, s32[16]{0:T(128)}, u32[]{:S(2)}) copy-start(s32[16]{0:T(128)} %param.13) | copy-start | bytes 196
  78.1 4.7 collective-permute-start.2
  81.3 5.4 %collective-permute-start.3 = (f32[18,1,1024]{2,0,1:T(8,128)S(1)}, f32[18,1,1024]{2,0,1:T(8,128)S(1)}, u32[]{:S(2)}, u32[]{:S(2)}) collective-permute-start(f32[18,1,1024]{2,0,1:T(8,128)S(1)} %copy.13), channel_id=1, source_target_pairs={{1,0},{2,1},{3,2},{4,3},{5,4},{6,5},{7,6},{8,7},{9,8},{10,9},{11,1... | collective-permute-start | bytes 221192 | tf_op jit(solution)/shard_map/ppermute | solution.py:24
  94.4 8.3 %copy-start.2 = (f32[16,64,1024]{2,1,0:T(8,128)S(1)}, f32[16,64,1024]{2,1,0:T(8,128)}, u32[]{:S(2)}) copy-start(f32[16,64,1024]{2,1,0:T(8,128)} %param.8) | copy-start | bytes 12582916
  124.4 20.8 %copy-start.7 = (s32[2048]{0:T(1024)S(1)}, s32[2048]{0:T(1024)}, u32[]{:S(2)}) copy-start(s32[2048]{0:T(1024)} %param.12) | copy-start | bytes 24580
  140.0 49.9 %collective-permute-start.4 = (f32[1,64,1024]{2,1,0:T(8,128)S(1)}, f32[1,64,1024]{2,1,0:T(8,128)S(1)}, u32[]{:S(2)}, u32[]{:S(2)}) collective-permute-start(f32[1,64,1024]{2,1,0:T(8,128)S(1)} %reshape.87), channel_id=1, source_target_pairs={{0,16},{16,32},{32,48},{48,64},{64,80},{80,96},{96,112},{1,17},{17... | collective-permute-start | bytes 786440 | tf_op jit(solution)/shard_map/ppermute | solution.py:22
  145.9 266.0 %all-to-all-start = ((s32[16,1,128]{2,1,0:T(1,128)}), s32[16,1,128]{2,1,0:T(1,128)S(1)}, u32[]{:S(2)}, u32[]{:S(2)}) async-start(s32[16,1,128]{2,1,0:T(1,128)} %bitcast.1), calls=%async_computation | async-start | bytes 16384 | tf_op jit(solution)/shard_map/all_to_all | solution.py:88
  159.2 33.6 %collective-permute-start.5 = (f32[1,64,1024]{2,1,0:T(8,128)S(1)}, f32[1,64,1024]{2,1,0:T(8,128)S(1)}, u32[]{:S(2)}, u32[]{:S(2)}) collective-permute-start(f32[1,64,1024]{2,1,0:T(8,128)S(1)} %reshape.88), channel_id=1, source_target_pairs={{16,0},{32,16},{48,32},{64,48},{80,64},{96,80},{112,96},{17,1},{33... | collective-permute-start | bytes 786440 | tf_op jit(solution)/shard_map/ppermute | solution.py:24
  192.9 4.9 collective-permute-start.6
  196.2 5.4 %collective-permute-start.7 = (f32[18,1,1024]{2,0,1:T(8,128)S(1)}, f32[18,1,1024]{2,0,1:T(8,128)S(1)}, u32[]{:S(2)}, u32[]{:S(2)}) collective-permute-start(f32[18,1,1024]{2,0,1:T(8,128)S(1)} %copy.19), channel_id=1, source_target_pairs={{1,0},{2,1},{3,2},{4,3},{5,4},{6,5},{7,6},{8,7},{9,8},{10,9},{11,1... | collective-permute-start | bytes 221192 | tf_op jit(solution)/shard_map/ppermute | solution.py:24
  209.1 10.5 %copy-start = (f32[16,64,1024]{2,1,0:T(8,128)S(1)}, f32[16,64,1024]{2,1,0:T(8,128)}, u32[]{:S(2)}) copy-start(f32[16,64,1024]{2,1,0:T(8,128)} %reshape.78) | copy-start | bytes 12582916
  209.1 10.5 %copy-start.3 = (f32[16,64,1024]{2,1,0:T(8,128)S(1)}, f32[16,64,1024]{2,1,0:T(8,128)}, u32[]{:S(2)}) copy-start(f32[16,64,1024]{2,1,0:T(8,128)} %param.8) | copy-start | bytes 12582916
  259.3 44.6 %collective-permute-start.8 = (f32[1,64,1024]{2,1,0:T(8,128)S(1)}, f32[1,64,1024]{2,1,0:T(8,128)S(1)}, u32[]{:S(2)}, u32[]{:S(2)}) collective-permute-start(f32[1,64,1024]{2,1,0:T(8,128)S(1)} %reshape.89), channel_id=1, source_target_pairs={{0,16},{16,32},{32,48},{48,64},{64,80},{80,96},{96,112},{1,17},{17... | collective-permute-start | bytes 786440 | tf_op jit(solution)/shard_map/ppermute | solution.py:22
  302.0 7.9 %collective-permute-start.9 = (f32[1,64,1024]{2,1,0:T(8,128)}, f32[1,64,1024]{2,1,0:T(8,128)S(1)}, u32[]{:S(2)}, u32[]{:S(2)}) collective-permute-start(f32[1,64,1024]{2,1,0:T(8,128)} %reshape.90), channel_id=1, source_target_pairs={{16,0},{32,16},{48,32},{64,48},{80,64},{96,80},{112,96},{17,1},{33... | collective-permute-start | bytes 786440 | tf_op jit(solution)/shard_map/ppermute | solution.py:24
  310.0 4.8 collective-permute-start.10
  313.1 5.4 %collective-permute-start.11 = (f32[18,1,1024]{2,0,1:T(8,128)S(1)}, f32[18,1,1024]{2,0,1:T(8,128)S(1)}, u32[]{:S(2)}, u32[]{:S(2)}) collective-permute-start(f32[18,1,1024]{2,0,1:T(8,128)S(1)} %copy.25), channel_id=1, source_target_pairs={{1,0},{2,1},{3,2},{4,3},{5,4},{6,5},{7,6},{8,7},{9,8},{10,9},{11,1... | collective-permute-start | bytes 221192 | tf_op jit(solution)/shard_map/ppermute | solution.py:24
  326.0 10.5 %copy-start.1 = (f32[16,64,1024]{2,1,0:T(8,128)S(1)}, f32[16,64,1024]{2,1,0:T(8,128)}, u32[]{:S(2)}) copy-start(f32[16,64,1024]{2,1,0:T(8,128)} %reshape.78) | copy-start | bytes 12582916
  326.0 10.5 %copy-start.4 = (f32[16,64,1024]{2,1,0:T(8,128)S(1)}, f32[16,64,1024]{2,1,0:T(8,128)}, u32[]{:S(2)}) copy-start(f32[16,64,1024]{2,1,0:T(8,128)} %reshape.82) | copy-start | bytes 12582916
  411.9 24.2 %all-to-all-start.1 = ((bf16[16,128,256]{2,1,0:T(8,128)(2,1)}), bf16[16,128,256]{2,1,0:T(8,128)(2,1)S(1)}, u32[]{:S(2)}, u32[]{:S(2)}) async-start(bf16[16,128,256]{2,1,0:T(8,128)(2,1)} %fusion.56), calls=%async_computation.1 | async-start | bytes 2097152 | tf_op jit(solution)/shard_map/all_to_all | solution.py:87
  420.8 75.9 %all-reduce.8.cloned.1.call-start = ((), (), s32[]{:S(2)}) async-start(), calls=%async_computation.2 | async-start | bytes 524288 | tf_op jit(solution)/shard_map/psum | solution.py:95
Sparse Core Ops, SparseCore 0:
  437.4 59.2 all-reduce.7
where the time goes:
time: 515 us; the launch traced here: 506 us
  local copies, waits for them, and re-layouts  210 us (41%)
  other arithmetic  138 us (27%)
  waiting for transfers between devices  89 us (17%)
  starting transfers between devices  52.2 us (10%)
  between operations  15 us (3%)
    gather x3, local copies, waits for them, and re-layouts, on_device(): updated[cell_z, cell_y, cell_x][:, None] * history[step].astype(jnp.float32)  86.4 us
    psum x1, waiting for transfers between devices, on_device(): gradient = lax.psum(partial_sum, 'slab')  59.4 us
    add x3, other arithmetic, on_device(): following = 2.0 * lam - prev + courant * laplace  54.6 us
    unnamed x6, other arithmetic  44.8 us
    add x3, other arithmetic, stencil(): side_side = side_x[:, :-2] + side_x[:, 2:]  29.3 us
    gather x1, local copies, waits for them, and re-layouts, on_device(): lam[cell_z, cell_y, cell_x] - prev[cell_z, cell_y, cell_x]  28.8 us
    gather x1, local copies, waits for them, and re-layouts, on_device(): prev[cell_z, cell_y, cell_x]  28.8 us
    unnamed x26, local copies, waits for them, and re-layouts  25.5 us
  transfers between devices with their start and end apart: 15, of which 7 were waited for; matrix products, arithmetic and copies ran while one was open for 58% of the time, Pallas kernels for 0%

commit v1 on v0

v1 whole, which is shorter than its diff:
```python
import jax
import jax.numpy as jnp
from jax import lax
from jax.experimental import pallas as pl
from jax.experimental.pallas import tpu as pltpu
from jax.sharding import PartitionSpec as P

PATCHES = 4096
CZ, CY, NX, LANES = 16, 64, 1024, 128
SUB = NX // LANES
SLOTS, K, STEPS = 2048, 256, 3
SLABS, TILES = 8, 16
CAP = SLOTS // TILES
OWN = PATCHES // TILES
MESH = pl.DeviceIdType.MESH
MIB = 1 << 20
NT = (((1,), (1,)), ((), ()))
DIRS = [(-1, 0), (1, 0), (-1, -1), (-1, 1), (1, -1), (1, 1), (0, -1), (0, 1)]


def damp_kernel(cell_s, count_s, cell_v, damp_v, keep, inc, old):
    def clear(i, carry):
        keep[pl.ds(pl.multiple_of(i * 64, 64), 64), :] = jnp.ones((64, LANES), jnp.float32)
        return carry

    lax.fori_loop(0, CZ * CY * SUB // 64, clear, 0)
    shape = (CAP, LANES)

    def block(j, carry):
        cell = cell_v[pl.ds(j, 1), :]
        damp = damp_v[pl.ds(j, 1), :]
        live = lax.broadcasted_iota(jnp.int32, (1, CAP), 1) < count_s[j]
        damp = jnp.where(live, damp, 0.0)
        row = jnp.broadcast_to((cell >> 7).astype(jnp.float32), shape)
        lane = jnp.broadcast_to(cell & 127, shape)
        same = jnp.where(row.T == row, jnp.broadcast_to(damp, shape), 0.0)
        onehot = (lane == lax.broadcasted_iota(jnp.int32, shape, 0)).astype(jnp.bfloat16)
        high = same.astype(jnp.bfloat16)
        rest = same - high.astype(jnp.float32)
        mid = rest.astype(jnp.bfloat16)
        low = (rest - mid.astype(jnp.float32)).astype(jnp.bfloat16)

        def place(part):
            return lax.dot_general(part, onehot, NT, preferred_element_type=jnp.float32)

        inc[...] = place(high) + place(mid) + place(low)
        base = pl.multiple_of(j * CAP, CAP)
        for k in range(CAP):
            old[pl.ds(k, 1), :] = keep[pl.ds(cell_s[base + k] >> 7, 1), :]
        inc[...] = old[...] - inc[...]
        for k in range(CAP):
            keep[pl.ds(cell_s[base + k] >> 7, 1), :] = inc[pl.ds(k, 1), :]
        return carry

    lax.fori_loop(0, TILES, block, 0)


def steps_kernel(
    adjoint, adjoint_prev, courant, keep, lam1, lam2, lam3,
    lam0, before, cour, load_sem, send_sem, recv_sem,
):
    slab, tile = lax.axis_index("slab"), lax.axis_index("tile")

    def chunk(src, dst, sem):
        for s in range(SUB):
            pltpu.make_async_copy(src.at[:, :, pl.ds(s * LANES, LANES)], dst.at[:, :, s, :], sem).start()

    inner = lam0.at[pl.ds(1, CZ), pl.ds(1, CY)]
    chunk(adjoint, inner, load_sem.at[0])
    chunk(adjoint_prev, before, load_sem.at[1])
    chunk(courant, cour, load_sem.at[2])

    def has(dz, dy):
        z, y = slab + dz, tile + dy
        return (z >= 0) & (z < SLABS) & (y >= 0) & (y < TILES)

    barrier = pltpu.get_barrier_semaphore()
    for dz, dy in DIRS:
        @pl.when(has(dz, dy))
        def _():
            pl.semaphore_signal(barrier, inc=1, device_id=(slab + dz, tile + dy), device_id_type=MESH)
    zs = jnp.where((slab == 0) | (slab == SLABS - 1), 2, 3)
    ys = jnp.where((tile == 0) | (tile == TILES - 1), 2, 3)

    for lam in (lam0, lam1, lam2):
        for at, there in ((0, slab == 0), (CZ + 1, slab == SLABS - 1)):
            @pl.when(there)
            def _():
                lam[at] = jnp.zeros((CY + 2, SUB, LANES), jnp.float32)
        for at, there in ((0, tile == 0), (CY + 1, tile == TILES - 1)):
            @pl.when(there)
            def _():
                for z in range(CZ + 2):
                    lam[z, at] = jnp.zeros((SUB, LANES), jnp.float32)
    pl.semaphore_wait(barrier, zs * ys - 1)

    def message(n, d):
        lam = (lam0, lam1, lam2)[n]
        dz, dy = DIRS[d]
        src_z = {-1: 1, 0: pl.ds(1, CZ), 1: CZ}[dz]
        dst_z = {-1: CZ + 1, 0: pl.ds(1, CZ), 1: 0}[dz]
        src_y = {-1: 1, 0: pl.ds(1, CY), 1: CY}[dy]
        dst_y = {-1: CY + 1, 0: pl.ds(1, CY), 1: 0}[dy]
        return pltpu.make_async_remote_copy(
            src_ref=lam.at[src_z, src_y],
            dst_ref=lam.at[dst_z, dst_y],
            send_sem=send_sem.at[n, d],
            recv_sem=recv_sem.at[n, d],
            device_id=(slab + dz, tile + dy),
            device_id_type=MESH,
        )

    def send(n, which):
        for d in which:
            @pl.when(has(*DIRS[d]))
            def _():
                message(n, d).start()

    def receive(n):
        for d in range(8):
            dz, dy = DIRS[d]
            @pl.when(has(-dz, -dy))
            def _():
                message(n, d).wait_recv()

    lane = lax.broadcasted_iota(jnp.int32, (SUB, LANES), 1)
    sub = lax.broadcasted_iota(jnp.int32, (SUB, LANES), 0)
    first_lane, last_lane = lane == 0, lane == LANES - 1
    not_first = jnp.where(sub == 0, 0.0, 1.0)
    not_last = jnp.where(sub == SUB - 1, 0.0, 1.0)

    def x_sides(q):
        left = pltpu.roll(q, 1, 1)
        right = pltpu.roll(q, LANES - 1, 1)
        left = jnp.where(first_lane, pltpu.roll(left, 1, 0) * not_first, left)
        right = jnp.where(last_lane, pltpu.roll(right, SUB - 1, 0) * not_last, right)
        return left + right

    def rows(n, z, first, count):
        lam = (lam0, lam1, lam2)[n]

        def parts(y):
            mid = lam[z, y]
            sides = lam[z - 1, y] + lam[z + 1, y]
            quarter = sides * 0.25
            a = mid + quarter
            b = (a + quarter) * 0.25
            return mid, sides, a, b

        down, here = parts(first - 1), parts(first)
        for k in range(count):
            y = first + k
            up = parts(y + 1)
            mid, sides, a, b = here
            q = a + (down[3] + up[3])
            twice = (sides - 10.0 * mid) + (down[2] + up[2]) + x_sides(q)
            prev = before[z - 1, y - 1] if n == 0 else (lam0, lam1)[n - 1][z, y]
            new = mid + (mid - prev) * keep[z - 1, y - 1] + cour[z - 1, y - 1] * (0.5 * twice)
            if n == 2:
                lam3[z - 1, y - 1] = new
            else:
                (lam1, lam2)[n][z, y] = new
            down, here = here, up

    half = (CY - 2) // 2

    def step(n):
        def inside(i, carry):
            rows(n, 2 + i // 2, 2 + (i % 2) * half, half)
            return carry

        lax.fori_loop(0, 2 * (CZ - 2), inside, 0)
        receive(n)

        def layer(i, carry):
            rows(n, 1 + (i // 2) * (CZ - 1), 1 + (i % 2) * (CY // 2), CY // 2)
            return carry

        lax.fori_loop(0, 4, layer, 0)
        if n < 2:
            send(n + 1, range(6))

        def edge(i, carry):
            rows(n, 2 + i, 1, 1)
            rows(n, 2 + i, CY, 1)
            return carry

        lax.fori_loop(0, CZ - 2, edge, 0)
        if n < 2:
            send(n + 1, range(6, 8))

    pltpu.make_async_copy(inner, inner, load_sem.at[0]).wait()
    send(0, range(8))
    pltpu.make_async_copy(before, before, load_sem.at[1]).wait()
    pltpu.make_async_copy(cour, cour, load_sem.at[2]).wait()
    for n in range(STEPS):
        step(n)
    for n in range(STEPS):
        for d in range(8):
            @pl.when(has(*DIRS[d]))
            def _():
                message(n, d).wait_send()


def rows_kernel(
    cell_s, count_s, cell_v, lam1, lam2, lam3, lam2_full, lam3_full, history,
    rows, final, previous, hist, got, out_sem, hist_sem,
):
    inner = lam2_full.at[pl.ds(1, CZ), pl.ds(1, CY)]
    copies = []
    for n in range(STEPS):
        pltpu.make_async_copy(history.at[n], hist.at[n], hist_sem.at[n]).start()
    for src, dst, sem in ((inner, previous, 0), (lam3_full, final, 1)):
        for s in range(SUB):
            copy = pltpu.make_async_copy(
                src.at[:, :, s, :], dst.at[:, :, pl.ds(s * LANES, LANES)], out_sem.at[sem, s]
            )
            copy.start()
            copies.append(copy)
    for n in range(STEPS):
        pltpu.make_async_copy(history.at[n], hist.at[n], hist_sem.at[n]).wait()
    shape = (CAP, LANES)

    def block(j, carry):
        base = pl.multiple_of(j * CAP, CAP)
        for k in range(CAP):
            cell = cell_s[base + k]
            flat = cell >> 7
            padded = flat + ((cell >> 16) << 4) + (CY + 3) * SUB
            got[0, pl.ds(k, 1), :] = lam1[pl.ds(padded, 1), :]
            got[1, pl.ds(k, 1), :] = lam2[pl.ds(padded, 1), :]
            got[2, pl.ds(k, 1), :] = lam3[pl.ds(flat, 1), :]
        lane = jnp.broadcast_to((cell_v[pl.ds(j, 1), :] & 127).astype(jnp.float32), shape).T
        here = lane.astype(jnp.int32) == lax.broadcasted_iota(jnp.int32, shape, 1)
        acc = jnp.zeros((CAP, K), jnp.float32)
        for n in range(STEPS):
            value = jnp.sum(jnp.where(here, got[n], 0.0), axis=1, keepdims=True)
            acc = acc + value * hist[n, pl.ds(base, CAP), :].astype(jnp.float32)
        live = lax.broadcasted_iota(jnp.int32, (CAP, K), 0) < count_s[j]
        rows[j] = jnp.where(live, acc, 0.0).astype(jnp.bfloat16)
        return carry

    lax.fori_loop(0, TILES, block, 0)
    for copy in copies:
        copy.wait()


def patch_kernel(
    rows, ids, out, got_rows, got_ids, total, chunks, result,
    id_send, id_recv, row_send, row_recv, part_send, part_recv, all_send, all_recv,
):
    slab, tile = lax.axis_index("slab"), lax.axis_index("tile")
    barrier = pltpu.get_barrier_semaphore()
    for k in range(1, TILES):
        pl.semaphore_signal(barrier, inc=1, device_id=(slab, (tile + k) % TILES), device_id_type=MESH)
    for k in range(1, SLABS):
        pl.semaphore_signal(barrier, inc=1, device_id=((slab + k) % SLABS, tile), device_id_type=MESH)
    pl.semaphore_wait(barrier, TILES + SLABS - 2)

    def to_tile(src, dst, send_sem, recv_sem, k):
        owner = (tile + k) % TILES
        return pltpu.make_async_remote_copy(
            src_ref=src.at[owner], dst_ref=dst.at[k], send_sem=send_sem.at[k], recv_sem=recv_sem.at[k],
            device_id=(slab, owner), device_id_type=MESH,
        )

    for k in range(1, TILES):
        to_tile(ids, got_ids, id_send, id_recv, k).start()
    for k in range(1, TILES):
        to_tile(rows, got_rows, row_send, row_recv, k).start()

    def summed(named, block):
        local = named - tile * OWN
        onehot = (
            jnp.broadcast_to(local, (OWN, CAP)) == lax.broadcasted_iota(jnp.int32, (OWN, CAP), 0)
        ).astype(jnp.bfloat16)
        return jnp.dot(onehot, block, preferred_element_type=jnp.float32)

    total[...] = summed(ids[tile], rows[tile])
    for k in range(1, TILES):
        to_tile(ids, got_ids, id_send, id_recv, k).wait_recv()
        to_tile(rows, got_rows, row_send, row_recv, k).wait_recv()
        total[...] += summed(got_ids[k], got_rows[k])

    part = OWN // SLABS
    mine = pl.ds(pl.multiple_of(slab * part, part), part)

    def to_slab(k):
        owner = (slab + k) % SLABS
        return pltpu.make_async_remote_copy(
            src_ref=total.at[pl.ds(pl.multiple_of(owner * part, part), part)], dst_ref=chunks.at[k],
            send_sem=part_send.at[k], recv_sem=part_recv.at[k], device_id=(owner, tile), device_id_type=MESH,
        )

    def to_all(k):
        return pltpu.make_async_remote_copy(
            src_ref=result.at[mine], dst_ref=result.at[mine],
            send_sem=all_send.at[k], recv_sem=all_recv.at[k],
            device_id=((slab + k) % SLABS, tile), device_id_type=MESH,
        )

    def from_all(k):
        owner = (slab + SLABS - k) % SLABS
        theirs = pl.ds(pl.multiple_of(owner * part, part), part)
        return pltpu.make_async_remote_copy(
            src_ref=result.at[mine], dst_ref=result.at[theirs],
            send_sem=all_send.at[k], recv_sem=all_recv.at[k],
            device_id=((slab + k) % SLABS, tile), device_id_type=MESH,
        )

    for k in range(1, SLABS):
        to_slab(k).start()
    mean = total[mine, :]
    for k in range(1, SLABS):
        to_slab(k).wait_recv()
        mean = mean + chunks[k]
    result[mine, :] = mean
    for k in range(1, SLABS):
        to_all(k).start()
    for k in range(1, SLABS):
        from_all(k).wait_recv()
    out[...] = result[...]
    for k in range(1, TILES):
        to_tile(ids, got_ids, id_send, id_recv, k).wait_send()
        to_tile(rows, got_rows, row_send, row_recv, k).wait_send()
    for k in range(1, SLABS):
        to_slab(k).wait_send()
        to_all(k).wait_send()


SMEM = pl.BlockSpec(memory_space=pltpu.SMEM)
VMEM = pl.BlockSpec(memory_space=pltpu.VMEM)
ANY = pl.BlockSpec(memory_space=pl.ANY)
F32, BF16, I32 = jnp.float32, jnp.bfloat16, jnp.int32
DMA = pltpu.SemaphoreType.DMA


def keep_in_vmem(array):
    return pltpu.with_memory_space_constraint(array, pltpu.VMEM)


def on_device(adjoint, adjoint_prev, courant, wall_cell, wall_patch, block_count, wall_damp, history):
    field = (CZ, CY, SUB, LANES)
    padded = (CZ + 2, CY + 2, SUB, LANES)
    cells = wall_cell.reshape(TILES, CAP)
    keep = pl.pallas_call(
        damp_kernel,
        out_shape=pltpu.VMEM((CZ * CY * SUB, LANES), F32),
        in_specs=[SMEM, SMEM, VMEM, VMEM],
        out_specs=VMEM,
        scratch_shapes=[pltpu.VMEM((CAP, LANES), F32)] * 2,
        compiler_params=pltpu.CompilerParams(vmem_limit_bytes=4 * MIB),
        name="damp",
    )(wall_cell, block_count, cells, wall_damp.reshape(TILES, CAP))
    keep = keep.reshape(field)
    lam1, lam2, lam3 = pl.pallas_call(
        steps_kernel,
        out_shape=(pltpu.VMEM(padded, F32), pltpu.VMEM(padded, F32), pltpu.VMEM(field, F32)),
        in_specs=[ANY, ANY, ANY, VMEM],
        out_specs=(VMEM, VMEM, VMEM),
        scratch_shapes=[
            pltpu.VMEM(padded, F32), pltpu.VMEM(field, F32), pltpu.VMEM(field, F32),
            DMA((3,)), DMA((3, 8)), DMA((3, 8)),
        ],
        compiler_params=pltpu.CompilerParams(
            vmem_limit_bytes=18 * MIB, collective_id=0, has_side_effects=True
        ),
        name="steps",
    )(adjoint, adjoint_prev, courant, keep_in_vmem(keep))
    flat1 = lam1.reshape(-1, LANES)
    flat2 = lam2.reshape(-1, LANES)
    flat3 = lam3.reshape(-1, LANES)
    rows, final, previous = pl.pallas_call(
        rows_kernel,
        out_shape=(
            jax.ShapeDtypeStruct((TILES, CAP, K), BF16),
            jax.ShapeDtypeStruct((CZ, CY, NX), F32),
            jax.ShapeDtypeStruct((CZ, CY, NX), F32),
        ),
        in_specs=[SMEM, SMEM, VMEM, VMEM, VMEM, VMEM, VMEM, VMEM, ANY],
        out_specs=(VMEM, ANY, ANY),
        scratch_shapes=[
            pltpu.VMEM((STEPS, SLOTS, K), BF16), pltpu.VMEM((STEPS, CAP, LANES), F32),
            DMA((2, SUB)), DMA((STEPS,)),
        ],
        compiler_params=pltpu.CompilerParams(vmem_limit_bytes=16 * MIB),
        name="rows",
    )(
        wall_cell, block_count, cells, keep_in_vmem(flat1), keep_in_vmem(flat2), keep_in_vmem(flat3),
        keep_in_vmem(lam2), keep_in_vmem(lam3), history,
    )
    part = OWN // SLABS
    gradient = pl.pallas_call(
        patch_kernel,
        out_shape=jax.ShapeDtypeStruct((OWN, K), F32),
        in_specs=[VMEM, VMEM],
        out_specs=VMEM,
        scratch_shapes=[
            pltpu.VMEM((TILES, CAP, K), BF16), pltpu.VMEM((TILES, 1, CAP), I32),
            pltpu.VMEM((OWN, K), F32), pltpu.VMEM((SLABS, part, K), F32), pltpu.VMEM((OWN, K), F32),
            DMA((TILES,)), DMA((TILES,)), DMA((TILES,)), DMA((TILES,)),
            DMA((SLABS,)), DMA((SLABS,)), DMA((SLABS,)), DMA((SLABS,)),
        ],
        compiler_params=pltpu.CompilerParams(
            vmem_limit_bytes=16 * MIB, collective_id=1, has_side_effects=True
        ),
        name="patch",
    )(rows, wall_patch.reshape(TILES, 1, CAP))
    return gradient, final, previous


def solution(mesh):
    return jax.shard_map(
        on_device,
        mesh=mesh,
        in_specs=(
            P("slab", "tile", None),
            P("slab", "tile", None),
            P("slab", "tile", None),
            P(("slab", "tile")),
            P(("slab", "tile")),
            P(("slab", "tile")),
            P(("slab", "tile")),
            P(None, ("slab", "tile"), None),
        ),
        out_specs=(P("tile", None), P("slab", "tile", None), P("slab", "tile", None)),
        check_vma=False,
    )
```

time: 515 us -> 90.9 us (0.18); the launches traced: 506 us -> 90.7 us
  local copies, waits for them, and re-layouts: 210 us -> 7.48 us
  other arithmetic: 138 us -> 0 us
  waiting for transfers between devices: 89 us -> 0 us
  Pallas kernels: 0 us -> 82.5 us
  starting transfers between devices: 52.2 us -> 0 us
  between operations: 15 us -> 0.74 us
    gather x5 -> x0, local copies, waits for them, and re-layouts: 144 us -> none  [the longest x3 86.4 us: on_device(): updated[cell_z, cell_y, cell_x][:, None] * history[step].astype(jnp.float32)]
    add x9 -> x0, other arithmetic: 86.5 us -> none  [the longest x3 54.6 us: on_device(): following = 2.0 * lam - prev + courant * laplace]
    pallas_call x0 -> x4, Pallas kernels: none -> 82.5 us  [the longest x1 33 us: on_device(): pl.pallas_call(patch_kernel, out_shape=jax.ShapeDtypeStruct((OWN, K), F32...]
    psum x1 -> x0, waiting for transfers between devices: 59.4 us -> none  [on_device(): gradient = lax.psum(partial_sum, 'slab')]
    unnamed x6 -> x0, other arithmetic: 44.8 us -> none
    ppermute x12 -> x0, starting transfers between devices: 34.9 us -> none  [the longest x6 24.7 us: extended(): lax.ppermute(tail, axis, [(i, (i + 1) % count) for i in range(ends)])]
    slice x20 -> x0, local copies, waits for them, and re-layouts: 25.2 us -> none  [the longest x3 17.6 us: x_sides(): from_right = jnp.concatenate([field[:, :, 1:], zero_col], axis=2)]
    unnamed x26 -> x21, local copies, waits for them, and re-layouts: 25.5 us -> 7.48 us
  transfers between devices with their start and end apart: 15 -> 0, of which waited for: 7 -> 0; matrix products, arithmetic and copies ran while one was open for 58% -> 0% of each run, Pallas kernels for 0% -> 0%
where the time goes in v1:
time: 90.9 us; the launch traced here: 90.7 us
  Pallas kernels  82.5 us (91%)
  local copies, waits for them, and re-layouts  7.48 us (8%)
    pallas_call x1, Pallas kernels, on_device(): pl.pallas_call(patch_kernel, out_shape=jax.ShapeDtypeStruct((OWN, K), F32...  33 us
    pallas_call x1, Pallas kernels, on_device(): pl.pallas_call(steps_kernel, out_shape=(pltpu.VMEM(padded, F32), pltpu.VM...  32.3 us
    pallas_call x1, Pallas kernels, on_device(): pl.pallas_call(damp_kernel, out_shape=pltpu.VMEM((CZ * CY * SUB, LANES),...  8.94 us
    pallas_call x1, Pallas kernels, on_device(): pl.pallas_call(rows_kernel, out_shape=(jax.ShapeDtypeStruct((TILES, CAP,...  8.21 us
    unnamed x21, local copies, waits for them, and re-layouts  7.48 us

profile of v1, /device:TPU:1, one launch (start us, length us, event | category | flops | bytes accessed | tf_op | source)
XLA Modules:
  0.0 90.7 jit_solution(14749599323935866245)
XLA Ops:
  0.6 0.0 copy-start
  0.6 0.0 copy-start.4
  0.7 0.8 copy-done.4
  1.5 0.0 copy-start.6
  1.5 0.9 copy-done.6
  2.4 0.0 copy-start.8
  2.4 0.7 copy-done.8
  3.0 8.9 %damp.1 = f32[8192,128]{1,0:T(8,128)S(1)} custom-call(s32[2048]{0:T(1024)S(1)} %copy-done.4, s32[16]{0:T(128)S(1)} %copy-done.8, s32[16,128]{1,0:T(8,128)S(1)} %bitcast.11, f32[16,128]{1,0:T(8,128)S(1)} %bitcast.13), custom_call_target="tpu_custom_call" | custom-call | tf_op jit(solution)/shard_map/damp/pallas_call | solution.py:346
  12.0 0.0 copy-done
  12.0 0.0 copy-start.1
  12.0 2.2 %copy-done.1 = f32[16,64,1024]{2,1,0:T(8,128)S(1)} copy-done((f32[16,64,1024]{2,1,0:T(8,128)S(1)}, f32[16,64,1024]{2,1,0:T(8,128)}, u32[]{:S(2)}) %copy-start.1) | copy-done | bytes 4194328
  14.2 0.0 copy-start.2
  14.2 2.2 %copy-done.2 = f32[16,64,1024]{2,1,0:T(8,128)S(1)} copy-done((f32[16,64,1024]{2,1,0:T(8,128)S(1)}, f32[16,64,1024]{2,1,0:T(8,128)}, u32[]{:S(2)}) %copy-start.2) | copy-done | bytes 4194328
  16.4 0.0 copy-start.3
  16.4 0.0 copy-start.5
  16.4 0.0 copy-start.9
  16.4 32.3 %steps.1 = (f32[18,66,8,128]{3,2,1,0:T(8,128)S(1)}, f32[18,66,8,128]{3,2,1,0:T(8,128)S(1)}, f32[16,64,8,128]{3,2,1,0:T(8,128)S(1)}) custom-call(f32[16,64,1024]{2,1,0:T(8,128)S(1)} %copy-done, f32[16,64,1024]{2,1,0:T(8,128)S(1)} %copy-done.1, f32[16,64,1024]{2,1,0:T(8,128)S(1)} %copy-done.2, f32[16,64,8,128]{3,2,1,0:T(8,128)S(1)} %bitcast.8), custom_call_target="tpu_custom_call" | custom-call | tf_op jit(solution)/shard_map/steps/pallas_call | solution.py:356
  48.7 0.0 copy-done.3
  48.7 0.0 copy-done.5
  48.7 0.0 copy-done.9
  48.7 0.0 copy-start.7
  48.7 8.2 %rows.1 = (bf16[16,128,256]{2,1,0:T(8,128)(2,1)S(1)}, f32[16,64,1024]{2,1,0:T(8,128)}, f32[16,64,1024]{2,1,0:T(8,128)}) custom-call(s32[2048]{0:T(1024)S(1)} %copy-done.5, s32[16]{0:T(128)S(1)} %copy-done.9, s32[16,128]{1,0:T(8,128)S(1)} %bitcast.12, f32[9504,128]{1,0:T(8,128)S(1)} %bitcast.10, f32[9504,128]{1,0:T(8,128)S(1)} %bitcast.7, ...), custom_call_target="tpu_custom_call" | custom-call | tf_op jit(solution)/shard_map/rows/pallas_call | solution.py:373
  56.9 0.0 copy-done.7
  57.0 33.0 %patch.1 = f32[256,256]{1,0:T(8,128)S(1)} custom-call(bf16[16,128,256]{2,1,0:T(8,128)(2,1)S(1)} %get-tuple-element.12.rows, s32[16,1,128]{2,1,0:T(1,128)S(1)} %bitcast.14), custom_call_target="tpu_custom_call" | custom-call | tf_op jit(solution)/shard_map/patch/pallas_call | solution.py:393
  90.0 0.7 copy.12
Async XLA Ops:
  0.6 11.4 %copy-start = (f32[16,64,1024]{2,1,0:T(8,128)S(1)}, f32[16,64,1024]{2,1,0:T(8,128)}, u32[]{:S(2)}) copy-start(f32[16,64,1024]{2,1,0:T(8,128)} %adjoint.1) | copy-start | bytes 12582916
  0.6 0.8 copy-start.4
  1.5 0.9 copy-start.6
  2.4 0.7 copy-start.8
  12.0 2.2 %copy-start.1 = (f32[16,64,1024]{2,1,0:T(8,128)S(1)}, f32[16,64,1024]{2,1,0:T(8,128)}, u32[]{:S(2)}) copy-start(f32[16,64,1024]{2,1,0:T(8,128)} %adjoint_prev.1) | copy-start | bytes 12582916
  14.2 2.2 %copy-start.2 = (f32[16,64,1024]{2,1,0:T(8,128)S(1)}, f32[16,64,1024]{2,1,0:T(8,128)}, u32[]{:S(2)}) copy-start(f32[16,64,1024]{2,1,0:T(8,128)} %courant.1) | copy-start | bytes 12582916
  16.4 32.3 %copy-start.3 = (bf16[3,2048,256]{2,1,0:T(8,128)(2,1)S(1)}, bf16[3,2048,256]{2,1,0:T(8,128)(2,1)}, u32[]{:S(2)}) copy-start(bf16[3,2048,256]{2,1,0:T(8,128)(2,1)} %history.1) | copy-start | bytes 9437188
  16.4 32.3 %copy-start.5 = (s32[2048]{0:T(1024)S(1)}, s32[2048]{0:T(1024)}, u32[]{:S(2)}) copy-start(s32[2048]{0:T(1024)} %cell_s.3) | copy-start | bytes 24580
  16.4 32.3 %copy-start.9 = (s32[16]{0:T(128)S(1)}, s32[16]{0:T(128)}, u32[]{:S(2)}) copy-start(s32[16]{0:T(128)} %count_s.3) | copy-start | bytes 196
  48.7 8.2 %copy-start.7 = (s32[2048]{0:T(1024)S(1)}, s32[2048]{0:T(1024)}, u32[]{:S(2)}) copy-start(s32[2048]{0:T(1024)} %param.12) | copy-start | bytes 24580

commit v2 on v0

v2 whole, which is shorter than its diff:
```python
import jax
import jax.numpy as jnp
from jax import lax
from jax.experimental import pallas as pl
from jax.experimental.pallas import tpu as pltpu
from jax.sharding import PartitionSpec as P

PATCHES = 4096
CZ, CY, NX, LANES = 16, 64, 1024, 128
SUB = NX // LANES
FLAT = CZ * CY * SUB
SLOTS, K, STEPS = 2048, 256, 3
SLABS, TILES, SIDE = 8, 16, 4
CAP = SLOTS // TILES
OWN = PATCHES // TILES
HALVES, WIDE = 2, 128
PART = OWN // SLABS
MESH = pl.DeviceIdType.MESH
MIB = 1 << 20
NT = (((1,), (1,)), ((), ()))
DIRS = [(-1, 0), (1, 0), (-1, -1), (-1, 1), (1, -1), (1, 1), (0, -1), (0, 1)]
OFFSETS = sorted(
    range(1, TILES),
    key=lambda k: -min(k // SIDE, SIDE - k // SIDE) - min(k % SIDE, SIDE - k % SIDE),
)
PICKS = SLOTS // CZ
EARLY = 8


def damp_kernel(
    count, cells, damps, adjoint, adjoint_prev, courant,
    keep, lam0, before, cour,
    row_s, count_s, cell_v, damp_v, row_v, inc, old, load_sem, small_sem,
):
    small = [(count, count_s), (cells, cell_v), (damps, damp_v)]
    for i, (src, dst) in enumerate(small):
        pltpu.make_async_copy(src, dst, small_sem.at[i]).start()
    for i, (src, dst) in enumerate(((adjoint, lam0), (adjoint_prev, before), (courant, cour))):
        for s in range(SUB):
            pltpu.make_async_copy(
                src.at[:, :, pl.ds(s * LANES, LANES)], dst.at[:, :, s, :], load_sem.at[i]
            ).start()

    def clear(i, carry):
        keep[pl.ds(pl.multiple_of(i * 128, 128), 128), :] = jnp.ones((128, LANES), jnp.float32)
        return carry

    lax.fori_loop(0, FLAT // 128, clear, 0)
    for i, (src, dst) in enumerate(small):
        pltpu.make_async_copy(src, dst, small_sem.at[i]).wait()
    row_v[...] = cell_v[...] >> 7
    table = pltpu.make_async_copy(row_v, row_s, small_sem.at[3])
    table.start()
    shape = (CAP, LANES)

    def loss(j, carry):
        cell = cell_v[pl.ds(j, 1), :]
        live = lax.broadcasted_iota(jnp.int32, (1, CAP), 1) < count_s[j]
        damp = jnp.where(live, damp_v[pl.ds(j, 1), :], 0.0)
        row = jnp.broadcast_to((cell >> 7).astype(jnp.float32), shape)
        lane = jnp.broadcast_to(cell & 127, shape)
        same = jnp.where(row.T == row, jnp.broadcast_to(damp, shape), 0.0)
        onehot = (lane == lax.broadcasted_iota(jnp.int32, shape, 0)).astype(jnp.bfloat16)
        high = same.astype(jnp.bfloat16)
        rest = same - high.astype(jnp.float32)
        mid = rest.astype(jnp.bfloat16)
        low = (rest - mid.astype(jnp.float32)).astype(jnp.bfloat16)

        def place(part):
            return lax.dot_general(part, onehot, NT, preferred_element_type=jnp.float32)

        inc[pl.ds(pl.multiple_of(j * CAP, CAP), CAP), :] = place(high) + place(mid) + place(low)
        return carry

    lax.fori_loop(0, TILES, loss, 0, unroll=4)
    table.wait()

    def block(j, carry):
        base = pl.multiple_of(j * CAP, CAP)
        for k in range(CAP):
            old[pl.ds(k, 1), :] = keep[pl.ds(row_s[j, k], 1), :]
        old[...] = old[...] - inc[pl.ds(base, CAP), :]
        for k in range(CAP):
            keep[pl.ds(row_s[j, k], 1), :] = old[pl.ds(k, 1), :]
        return carry

    lax.fori_loop(0, TILES, block, 0)
    for i, dst in enumerate((lam0, before, cour)):
        pltpu.make_async_copy(dst, dst, load_sem.at[i]).wait()


def stepper(lam, layer_z, layer_y, before, keep, cour, out, cell_s=None, got=None):
    lane = lax.broadcasted_iota(jnp.int32, (SUB, LANES), 1)
    sub = lax.broadcasted_iota(jnp.int32, (SUB, LANES), 0)
    first_lane, last_lane = lane == 0, lane == LANES - 1
    not_first = jnp.where(sub == 0, 0.0, 1.0)
    not_last = jnp.where(sub == SUB - 1, 0.0, 1.0)
    flat = lam.reshape(FLAT, LANES) if got is not None else None

    def x_sides(q):
        left = pltpu.roll(q, 1, 1)
        right = pltpu.roll(q, LANES - 1, 1)
        left = jnp.where(first_lane, pltpu.roll(left, 1, 0) * not_first, left)
        right = jnp.where(last_lane, pltpu.roll(right, SUB - 1, 0) * not_last, right)
        return left + right

    def cells(z, y):
        if isinstance(z, int) and not 0 <= z < CZ:
            return layer_z[int(z > 0), y + 1]
        if isinstance(y, int) and not 0 <= y < CY:
            return layer_y[int(y > 0), z]
        return lam[z, y]

    def rows(z, first, count, picks=None):
        def parts(y):
            mid = cells(z, y)
            sides = cells(z - 1, y) + cells(z + 1, y)
            quarter = sides * 0.25
            a = mid + quarter
            return mid, sides, a, (a + quarter) * 0.25

        down, here = parts(first - 1), parts(first)
        for k in range(count):
            y = first + k
            up = parts(y + 1)
            mid, sides, a, b = here
            q = a + (down[3] + up[3])
            twice = (sides - 10.0 * mid) + (down[2] + up[2]) + x_sides(q)
            out[z, y] = mid + (mid - before[z, y]) * keep[z, y] + cour[z, y] * (0.5 * twice)
            down, here = here, up
            if got is not None and picks is not None:
                for slot in range(PICKS * k // count, PICKS * (k + 1) // count):
                    at = picks * PICKS + slot
                    got[pl.ds(at, 1), :] = flat[pl.ds(cell_s[at] >> 7, 1), :]

    def inside(first, last):
        def layer(z, carry):
            rows(z, 1, CY - 2, z)
            return carry

        lax.fori_loop(first, last + 1, layer, 0)

    def layers():
        for z in (0, CZ - 1):
            rows(z, 0, CY, z)

    def edges():
        def edge(i, carry):
            for k in range(7):
                rows(1 + 7 * i + k, 0, 1)
                rows(1 + 7 * i + k, CY - 1, 1)
            return carry

        lax.fori_loop(0, (CZ - 2) // 7, edge, 0)

    return inside, layers, edges


def steps_kernel(
    lam0, before, cour, keep, cell,
    lam1, lam2, lam3, last_z, last_y, got1, got2,
    layer_z, layer_y, cell_s, cell_sem, send_sem, recv_sem,
):
    slab, tile = lax.axis_index("slab"), lax.axis_index("tile")

    def has(dz, dy):
        z, y = slab + dz, tile + dy
        return (z >= 0) & (z < SLABS) & (y >= 0) & (y < TILES)

    barrier = pltpu.get_barrier_semaphore()
    for dz, dy in DIRS:
        @pl.when(has(dz, dy))
        def _():
            pl.semaphore_signal(barrier, inc=1, device_id=(slab + dz, tile + dy), device_id_type=MESH)
    zs = jnp.where((slab == 0) | (slab == SLABS - 1), 2, 3)
    ys = jnp.where((tile == 0) | (tile == TILES - 1), 2, 3)
    pltpu.make_async_copy(cell, cell_s, cell_sem).start()
    lams = (lam0, lam1, lam2)
    zlayers = (layer_z.at[0], layer_z.at[1], last_z)
    ylayers = (layer_y.at[0], layer_y.at[1], last_y)

    for n in range(STEPS):
        for side, no_z, no_y in ((0, slab == 0, tile == 0), (1, slab == SLABS - 1, tile == TILES - 1)):
            @pl.when(no_z)
            def _():
                zlayers[n][side] = jnp.zeros((CY + 2, SUB, LANES), jnp.float32)
            @pl.when(no_y)
            def _():
                ylayers[n][side] = jnp.zeros((CZ, SUB, LANES), jnp.float32)
                for z in range(2):
                    zlayers[n][z, side * (CY + 1)] = jnp.zeros((SUB, LANES), jnp.float32)

    def message(n, d):
        dz, dy = DIRS[d]
        src_z = {-1: 0, 0: pl.ds(0, CZ), 1: CZ - 1}[dz]
        src_y = {-1: 0, 0: pl.ds(0, CY), 1: CY - 1}[dy]
        if dz:
            dst = zlayers[n].at[int(dz < 0), {-1: CY + 1, 0: pl.ds(1, CY), 1: 0}[dy]]
        else:
            dst = ylayers[n].at[int(dy < 0)]
        return pltpu.make_async_remote_copy(
            src_ref=lams[n].at[src_z, src_y],
            dst_ref=dst,
            send_sem=send_sem.at[n, d],
            recv_sem=recv_sem.at[n, d],
            device_id=(slab + dz, tile + dy),
            device_id_type=MESH,
        )

    def send(n, which):
        for d in which:
            @pl.when(has(*DIRS[d]))
            def _():
                message(n, d).start()

    def receive(n):
        for d in range(8):
            dz, dy = DIRS[d]
            @pl.when(has(-dz, -dy))
            def _():
                message(n, d).wait_recv()

    first = stepper(lam0, zlayers[0], ylayers[0], before, keep, cour, lam1)
    second = stepper(lam1, zlayers[1], ylayers[1], lam0, keep, cour, lam2, cell_s, got1)
    third = stepper(lam2, zlayers[2], ylayers[2], lam1, keep, cour, lam3, cell_s, got2)

    def outer(n, step):
        receive(n - 1)
        step[1]()
        send(n, range(6))
        step[2]()
        send(n, range(6, 8))

    first[0](1, 5)
    pl.semaphore_wait(barrier, zs * ys - 1)
    send(0, range(8))
    first[0](6, CZ - 2)
    outer(1, first)
    pltpu.make_async_copy(cell, cell_s, cell_sem).wait()
    second[0](1, CZ - 2)
    outer(2, second)
    third[0](1, EARLY)
    receive(2)
    for n in range(STEPS):
        for d in range(8):
            @pl.when(has(*DIRS[d]))
            def _():
                message(n, d).wait_send()


def last_kernel(
    lam1, lam2, begun, begun2, layer_z, layer_y, keep, cour, cell,
    lam3, final, previous, got2,
    cell_s, cell_sem, out_sem,
):
    del begun, begun2

    def writes(src, dst, first, count, sem):
        return [
            pltpu.make_async_copy(
                src.at[pl.ds(first, count), :, s, :],
                dst.at[pl.ds(first, count), :, pl.ds(s * LANES, LANES)],
                out_sem.at[sem, s],
            )
            for s in range(SUB)
        ]

    copies = writes(lam2, previous, 0, CZ, 0)
    pltpu.make_async_copy(cell, cell_s, cell_sem).start()
    for copy in copies:
        copy.start()
    pltpu.make_async_copy(cell, cell_s, cell_sem).wait()
    inside, layers, edges = stepper(lam2, layer_z, layer_y, lam1, keep, cour, lam3, cell_s, got2)

    edges()
    layers()
    done = 1 + EARLY
    head = writes(lam3, final, 0, done, 1)
    for copy in head:
        copy.start()
    inside(done, CZ - 2)
    tail = writes(lam3, final, done, CZ - done, 2)
    for copy in tail:
        copy.start()
    for copy in copies + head + tail:
        copy.wait()


def patch_kernel(
    cell, count, ids, cells, lam3, got1, got2, history,
    out,
    cell_s, count_s, stage, got_rows, got_ids, onehots, got3, total, chunks, result,
    small_sem, id_send, id_recv, row_send, row_recv, part_send, part_recv, all_send, all_recv,
):
    slab, tile = lax.axis_index("slab"), lax.axis_index("tile")
    barrier = pltpu.get_barrier_semaphore()
    for k in range(1, TILES):
        pl.semaphore_signal(barrier, inc=1, device_id=(slab, (tile + k) % TILES), device_id_type=MESH)
    for k in range(1, SLABS):
        pl.semaphore_signal(barrier, inc=1, device_id=((slab + k) % SLABS, tile), device_id_type=MESH)
    small = [(cell, cell_s), (count, count_s)]
    for i, (src, dst) in enumerate(small):
        pltpu.make_async_copy(src, dst, small_sem.at[i]).start()
    for i, (src, dst) in enumerate(small):
        pltpu.make_async_copy(src, dst, small_sem.at[i]).wait()
    shape = (CAP, LANES)

    def owner_of(k):
        return (((tile >> 2) + k // SIDE) & 3) * SIDE + ((tile + k) & 3)

    def ids_to(k):
        owner = owner_of(k)
        return pltpu.make_async_remote_copy(
            src_ref=ids.at[owner], dst_ref=got_ids.at[k], send_sem=id_send.at[k], recv_sem=id_recv.at[k],
            device_id=(slab, owner), device_id_type=MESH,
        )

    def rows_to(k, h):
        return pltpu.make_async_remote_copy(
            src_ref=stage.at[h, k], dst_ref=got_rows.at[h, k],
            send_sem=row_send.at[h, k], recv_sem=row_recv.at[h, k],
            device_id=(slab, owner_of(k)), device_id_type=MESH,
        )

    def make_rows(k):
        j = owner_of(k)
        base = pl.multiple_of(j * CAP, CAP)
        for i in range(CAP):
            got3[pl.ds(i, 1), :] = lam3[pl.ds(cell_s[base + i] >> 7, 1), :]
        lane = jnp.broadcast_to((cells[pl.ds(j, 1), :] & 127).astype(jnp.float32), shape).T
        here = lane.astype(jnp.int32) == lax.broadcasted_iota(jnp.int32, shape, 1)
        acc = jnp.zeros((CAP, K), jnp.float32)
        for n, got in enumerate((got1[pl.ds(base, CAP), :], got2[pl.ds(base, CAP), :], got3[...])):
            value = jnp.sum(jnp.where(here, got, 0.0), axis=1, keepdims=True)
            acc = acc + value * history[n, pl.ds(base, CAP), :].astype(jnp.float32)
        live = lax.broadcasted_iota(jnp.int32, (CAP, K), 0) < count_s[j]
        acc = jnp.where(live, acc, 0.0).astype(jnp.bfloat16)
        for h in range(HALVES):
            stage[h, k] = acc[:, h * WIDE:(h + 1) * WIDE]

    def onehot_of(named):
        return (
            jnp.broadcast_to(named - tile * OWN, (OWN, CAP)) == lax.broadcasted_iota(jnp.int32, (OWN, CAP), 0)
        ).astype(jnp.bfloat16)

    for k in OFFSETS:
        make_rows(k)
    pl.semaphore_wait(barrier, TILES + SLABS - 2)
    for k in OFFSETS:
        ids_to(k).start()
    for h in range(HALVES):
        for k in OFFSETS:
            rows_to(k, h).start()
    make_rows(0)
    onehots[0] = onehot_of(ids[tile])
    for h in range(HALVES):
        total[h] = jnp.dot(onehots[0], stage[h, 0], preferred_element_type=jnp.float32)
    for k in OFFSETS:
        ids_to(k).wait_recv()
        onehots[k] = onehot_of(got_ids[k])

    mine = pl.ds(pl.multiple_of(slab * PART, PART), PART)

    def to_slab(k, h):
        owner = (slab + k) % SLABS
        return pltpu.make_async_remote_copy(
            src_ref=total.at[h, pl.ds(pl.multiple_of(owner * PART, PART), PART)], dst_ref=chunks.at[h, k],
            send_sem=part_send.at[h, k], recv_sem=part_recv.at[h, k],
            device_id=(owner, tile), device_id_type=MESH,
        )

    def to_all(k, h, back=False):
        owner = (slab + SLABS - k) % SLABS if back else slab
        return pltpu.make_async_remote_copy(
            src_ref=result.at[h, mine],
            dst_ref=result.at[h, pl.ds(pl.multiple_of(owner * PART, PART), PART)],
            send_sem=all_send.at[h, k], recv_sem=all_recv.at[h, k],
            device_id=((slab + k) % SLABS, tile), device_id_type=MESH,
        )

    def add_rows(h, which):
        for k in which:
            rows_to(k, h).wait_recv()
            total[h] += jnp.dot(onehots[k], got_rows[h, k], preferred_element_type=jnp.float32)

    def spread(h):
        for k in range(1, SLABS):
            to_slab(k, h).start()

    def gather(h):
        whole = total[h, mine, :]
        for k in range(1, SLABS):
            to_slab(k, h).wait_recv()
            whole = whole + chunks[h, k]
        result[h, mine, :] = whole
        for k in range(1, SLABS):
            to_all(k, h).start()

    add_rows(0, OFFSETS)
    spread(0)
    add_rows(1, OFFSETS[:10])
    gather(0)
    add_rows(1, OFFSETS[10:])
    spread(1)
    gather(1)
    for h in range(HALVES):
        for k in range(1, SLABS):
            to_all(k, h, True).wait_recv()
        out[:, h * WIDE:(h + 1) * WIDE] = result[h]
    for k in OFFSETS:
        ids_to(k).wait_send()
        for h in range(HALVES):
            rows_to(k, h).wait_send()
    for h in range(HALVES):
        for k in range(1, SLABS):
            to_slab(k, h).wait_send()
            to_all(k, h).wait_send()


SMEM = pl.BlockSpec(memory_space=pltpu.SMEM)
VMEM = pl.BlockSpec(memory_space=pltpu.VMEM)
HBM = pl.BlockSpec(memory_space=pltpu.HBM)
F32, BF16, I32 = jnp.float32, jnp.bfloat16, jnp.int32
DMA = pltpu.SemaphoreType.DMA
FIELD = (CZ, CY, SUB, LANES)


def in_vmem(*arrays):
    return [pltpu.with_memory_space_constraint(array, pltpu.VMEM) for array in arrays]


def in_hbm(*arrays):
    return [pltpu.with_memory_space_constraint(array, pltpu.HBM) for array in arrays]


def on_device(adjoint, adjoint_prev, courant, wall_cell, wall_patch, block_count, wall_damp, history):
    field = pltpu.VMEM(FIELD, F32)
    picked = pltpu.VMEM((SLOTS, LANES), F32)
    cells = wall_cell.reshape(TILES, CAP)
    damps = wall_damp.reshape(TILES, CAP)
    cell_s, count_s = pltpu.SMEM((SLOTS,), I32), pltpu.SMEM((TILES,), I32)
    keep, lam0, before, cour = pl.pallas_call(
        damp_kernel,
        out_shape=(pltpu.VMEM((FLAT, LANES), F32), field, field, field),
        in_specs=[HBM] * 6,
        out_specs=(VMEM,) * 4,
        scratch_shapes=[
            pltpu.SMEM((TILES, CAP), I32), count_s,
            pltpu.VMEM((TILES, CAP), I32), pltpu.VMEM((TILES, CAP), F32), pltpu.VMEM((TILES, CAP), I32),
            picked, pltpu.VMEM((CAP, LANES), F32), DMA((3,)), DMA((4,)),
        ],
        compiler_params=pltpu.CompilerParams(vmem_limit_bytes=4 * MIB),
        name="damp",
    )(*in_hbm(block_count, cells, damps, adjoint, adjoint_prev, courant))
    keep = keep.reshape(FIELD)
    zlayer, ylayer = (2, CY + 2, SUB, LANES), (2, CZ, SUB, LANES)
    lam1, lam2, begun, layer_z, layer_y, got1, begun2 = pl.pallas_call(
        steps_kernel,
        out_shape=(field, field, field, pltpu.VMEM(zlayer, F32), pltpu.VMEM(ylayer, F32), picked, picked),
        in_specs=[VMEM] * 4 + [HBM],
        out_specs=(VMEM,) * 7,
        scratch_shapes=[
            pltpu.VMEM((2, *zlayer), F32), pltpu.VMEM((2, *ylayer), F32), cell_s,
            DMA, DMA((3, 8)), DMA((3, 8)),
        ],
        compiler_params=pltpu.CompilerParams(
            vmem_limit_bytes=5 * MIB, collective_id=0, has_side_effects=True
        ),
        name="steps",
    )(*in_vmem(lam0, before, cour, keep), *in_hbm(wall_cell))
    whole = jax.ShapeDtypeStruct((CZ, CY, NX), F32)
    lam3, final, previous, got2 = pl.pallas_call(
        last_kernel,
        out_shape=(field, whole, whole, picked),
        in_specs=[VMEM] * 8 + [HBM],
        out_specs=(VMEM, HBM, HBM, VMEM),
        scratch_shapes=[cell_s, DMA, DMA((3, SUB))],
        input_output_aliases={2: 0, 3: 3},
        compiler_params=pltpu.CompilerParams(vmem_limit_bytes=4 * MIB),
        name="last",
    )(*in_vmem(lam1, lam2, begun, begun2, layer_z, layer_y, keep, cour), *in_hbm(wall_cell))
    gradient = pl.pallas_call(
        patch_kernel,
        out_shape=jax.ShapeDtypeStruct((OWN, K), F32),
        in_specs=[HBM, HBM] + [VMEM] * 6,
        out_specs=VMEM,
        scratch_shapes=[
            cell_s, count_s,
            pltpu.VMEM((HALVES, TILES, CAP, WIDE), BF16), pltpu.VMEM((HALVES, TILES, CAP, WIDE), BF16),
            pltpu.VMEM((TILES, 1, CAP), I32), pltpu.VMEM((TILES, OWN, CAP), BF16), pltpu.VMEM((CAP, LANES), F32),
            pltpu.VMEM((HALVES, OWN, WIDE), F32), pltpu.VMEM((HALVES, SLABS, PART, WIDE), F32),
            pltpu.VMEM((HALVES, OWN, WIDE), F32),
            DMA((2,)), DMA((TILES,)), DMA((TILES,)), DMA((HALVES, TILES)), DMA((HALVES, TILES)),
            DMA((HALVES, SLABS)), DMA((HALVES, SLABS)), DMA((HALVES, SLABS)), DMA((HALVES, SLABS)),
        ],
        compiler_params=pltpu.CompilerParams(
            vmem_limit_bytes=8 * MIB, collective_id=1, has_side_effects=True
        ),
        name="patch",
    )(
        *in_hbm(wall_cell, block_count),
        wall_patch.reshape(TILES, 1, CAP), cells,
        *in_vmem(lam3.reshape(FLAT, LANES), got1, got2), history,
    )
    return gradient, final, previous


def solution(mesh):
    return jax.shard_map(
        on_device,
        mesh=mesh,
        in_specs=(
            P("slab", "tile", None),
            P("slab", "tile", None),
            P("slab", "tile", None),
            P(("slab", "tile")),
            P(("slab", "tile")),
            P(("slab", "tile")),
            P(("slab", "tile")),
            P(None, ("slab", "tile"), None),
        ),
        out_specs=(P("tile", None), P("slab", "tile", None), P("slab", "tile", None)),
        check_vma=False,
    )
```

time: 515 us -> 65.1 us (0.13); the launches traced: 506 us -> 64.8 us
  local copies, waits for them, and re-layouts: 210 us -> 0.72 us
  other arithmetic: 138 us -> 0 us
  waiting for transfers between devices: 89 us -> 0 us
  Pallas kernels: 0 us -> 63.4 us
  starting transfers between devices: 52.2 us -> 0 us
  between operations: 15 us -> 0.69 us
    gather x5 -> x0, local copies, waits for them, and re-layouts: 144 us -> none  [the longest x3 86.4 us: on_device(): updated[cell_z, cell_y, cell_x][:, None] * history[step].astype(jnp.float32)]
    add x9 -> x0, other arithmetic: 86.5 us -> none  [the longest x3 54.6 us: on_device(): following = 2.0 * lam - prev + courant * laplace]
    pallas_call x0 -> x4, Pallas kernels: none -> 63.4 us  [the longest x1 32.5 us: on_device(): pl.pallas_call(patch_kernel, out_shape=jax.ShapeDtypeStruct((OWN, K), F32...]
    psum x1 -> x0, waiting for transfers between devices: 59.4 us -> none  [on_device(): gradient = lax.psum(partial_sum, 'slab')]
    unnamed x6 -> x0, other arithmetic: 44.8 us -> none
    ppermute x12 -> x0, starting transfers between devices: 34.9 us -> none  [the longest x6 24.7 us: extended(): lax.ppermute(tail, axis, [(i, (i + 1) % count) for i in range(ends)])]
    slice x20 -> x0, local copies, waits for them, and re-layouts: 25.2 us -> none  [the longest x3 17.6 us: x_sides(): from_right = jnp.concatenate([field[:, :, 1:], zero_col], axis=2)]
    unnamed x26 -> x5, local copies, waits for them, and re-layouts: 25.5 us -> 0.72 us
  transfers between devices with their start and end apart: 15 -> 0, of which waited for: 7 -> 0; matrix products, arithmetic and copies ran while one was open for 58% -> 0% of each run, Pallas kernels for 0% -> 0%
where the time goes in v2:
time: 65.1 us; the launch traced here: 64.8 us
  Pallas kernels  63.4 us (97%)
  local copies, waits for them, and re-layouts  0.72 us (1%)
  between operations  0.69 us (1%)
    pallas_call x1, Pallas kernels, on_device(): pl.pallas_call(patch_kernel, out_shape=jax.ShapeDtypeStruct((OWN, K), F32...  32.5 us
    pallas_call x1, Pallas kernels, on_device(): pl.pallas_call(steps_kernel, out_shape=(field, field, field, pltpu.VMEM(z...  20.2 us
    pallas_call x1, Pallas kernels, on_device(): pl.pallas_call(damp_kernel, out_shape=(pltpu.VMEM((FLAT, LANES), F32), fi...  5.93 us
    pallas_call x1, Pallas kernels, on_device(): pl.pallas_call(last_kernel, out_shape=(field, whole, whole, picked), in_s...  4.82 us

profile of v2, /device:TPU:1, one launch (start us, length us, event | category | flops | bytes accessed | tf_op | source)
XLA Modules:
  0.0 64.8 jit_solution(9156130585919087268)
XLA Ops:
  0.6 5.9 %damp.1 = (f32[8192,128]{1,0:T(8,128)S(1)}, f32[16,64,8,128]{3,2,1,0:T(8,128)S(1)}, f32[16,64,8,128]{3,2,1,0:T(8,128)S(1)}, f32[16,64,8,128]{3,2,1,0:T(8,128)S(1)}) custom-call(s32[16]{0:T(128)} %count.3, s32[16,128]{1,0:T(8,128)} %bitcast.9, f32[16,128]{1,0:T(8,128)} %bitcast.11, f32[16,64,1024]{2,1,0:T(8,128)} %adjoint.1, f32[16,64,1024]{2,1,0:T(8,128)} %adjoint_prev.1, ...), custom_call_target="tpu_custom_call" | custom-call | tf_op jit(solution)/shard_map/damp/pallas_call | solution.py:442
  6.6 20.2 %steps.1 = (f32[16,64,8,128]{3,2,1,0:T(8,128)S(1)}, f32[16,64,8,128]{3,2,1,0:T(8,128)S(1)}, f32[16,64,8,128]{3,2,1,0:T(8,128)S(1)}, f32[2,66,8,128]{3,2,1,0:T(8,...) custom-call(f32[16,64,8,128]{3,2,1,0:T(8,128)S(1)} %get-tuple-element.18.lam0, ...), custom_call_target="tpu_custom_call" | custom-call | tf_op jit(solution)/shard_map/steps/pallas_call | solution.py:457
  26.8 0.0 copy-start
  26.8 0.0 copy-start.1
  26.8 4.8 %last.1 = (f32[16,64,8,128]{3,2,1,0:T(8,128)S(1)}, f32[16,64,1024]{2,1,0:T(8,128)}, f32[16,64,1024]{2,1,0:T(8,128)}, f32[2048,128]{1,0:T(8,128)S(1)}) custom-call(f32[16,64,8,128]{3,2,1,0:T(8,128)S(1)} %get-tuple-element.22.lam1, f32[16,64,8,128]{3,2,1,0:T(8,128)S(1)} %get-tuple-element.23.lam2, ...), custom_call_target="tpu_custom_call", output_to_operand_aliasing={{0}: (2, {}), {3}: (3, {})} | custom-call | tf_op jit(solution)/shard_map/last/pallas_call | solution.py:472
  31.6 0.0 copy-done
  31.6 0.0 copy-done.1
  31.6 32.5 %patch.1 = f32[256,256]{1,0:T(8,128)S(1)} custom-call(s32[2048]{0:T(1024)} %cell.5, s32[16]{0:T(128)} %count.3, s32[16,1,128]{2,1,0:T(1,128)S(1)} %bitcast.8, s32[16,128]{1,0:T(8,128)} %bitcast.10, f32[8192,128]{1,0:T(8,128)S(1)} %bitcast.5, f32[2048,128]{1,0:T(8,128)S(1)} %get-tuple-element.29.got1, f32[2048,128]{1,0:T(8,128)S(1)} %get-tuple-element.30.got2, ...), custom_call_target="tpu_custom_call" | custom-call | tf_op jit(solution)/shard_map/patch/pallas_call | solution.py:482
  64.1 0.7 %copy.16 = f32[256,256]{1,0:T(8,128)} copy(f32[256,256]{1,0:T(8,128)S(1)} %patch.1) | data formatting | bytes 524288
Async XLA Ops:
  26.8 4.8 %copy-start = (bf16[3,2048,256]{2,1,0:T(8,128)(2,1)S(1)}, bf16[3,2048,256]{2,1,0:T(8,128)(2,1)}, u32[]{:S(2)}) copy-start(bf16[3,2048,256]{2,1,0:T(8,128)(2,1)} %history.1) | copy-start | bytes 9437188
  26.8 4.8 %copy-start.1 = (s32[2048]{0:T(1024)S(1)}, s32[2048]{0:T(1024)}, u32[]{:S(2)}) copy-start(s32[2048]{0:T(1024)} %param.12) | copy-start | bytes 24580

commit v3 on v2

--- a/solution.py
+++ b/solution.py
@@ -24,7 +24,6 @@
     key=lambda k: -min(k // SIDE, SIDE - k // SIDE) - min(k % SIDE, SIDE - k % SIDE),
 )
 PICKS = SLOTS // CZ
-EARLY = 8
 
 
 def damp_kernel(
@@ -156,10 +155,12 @@
     return inside, layers, edges
 
 
-def steps_kernel(
-    lam0, before, cour, keep, cell,
-    lam1, lam2, lam3, last_z, last_y, got1, got2,
-    layer_z, layer_y, cell_s, cell_sem, send_sem, recv_sem,
+def wave_kernel(
+    lam0, before, cour, keep, cell, count, cells, ids, history,
+    lam2, lam3, out,
+    lam1, layer_z, layer_y, sent_z, sent_y, came_z, came_y, got1, got2, got3, cell_s, count_s, cell_v, id_v, hist,
+    stage, got_rows, got_ids, onehots, total, chunks, result,
+    load_sem, send_sem, recv_sem, id_send, id_recv, row_send, row_recv, part_send, part_recv, all_send, all_recv,
 ):
     slab, tile = lax.axis_index("slab"), lax.axis_index("tile")
 
@@ -168,16 +169,23 @@
         return (z >= 0) & (z < SLABS) & (y >= 0) & (y < TILES)
 
     barrier = pltpu.get_barrier_semaphore()
-    for dz, dy in DIRS:
+    for dz, dy in DIRS[2:6]:
         @pl.when(has(dz, dy))
         def _():
             pl.semaphore_signal(barrier, inc=1, device_id=(slab + dz, tile + dy), device_id_type=MESH)
-    zs = jnp.where((slab == 0) | (slab == SLABS - 1), 2, 3)
-    ys = jnp.where((tile == 0) | (tile == TILES - 1), 2, 3)
-    pltpu.make_async_copy(cell, cell_s, cell_sem).start()
+    for k in range(1, SLABS):
+        pl.semaphore_signal(barrier, inc=1, device_id=((slab + k) % SLABS, tile), device_id_type=MESH)
+    for k in range(1, TILES):
+        pl.semaphore_signal(barrier, inc=1, device_id=(slab, (tile + k) % TILES), device_id_type=MESH)
+    zs = jnp.where((slab == 0) | (slab == SLABS - 1), 1, 2)
+    ys = jnp.where((tile == 0) | (tile == TILES - 1), 1, 2)
+    loads = [(cell, cell_s), (count, count_s), (cells, cell_v), (ids, id_v), (history, hist)]
+    loads = [pltpu.make_async_copy(src, dst, load_sem.at[i]) for i, (src, dst) in enumerate(loads)]
+    for load in loads:
+        load.start()
     lams = (lam0, lam1, lam2)
-    zlayers = (layer_z.at[0], layer_z.at[1], last_z)
-    ylayers = (layer_y.at[0], layer_y.at[1], last_y)
+    zlayers = [layer_z.at[n] for n in range(STEPS)]
+    ylayers = [layer_y.at[n] for n in range(STEPS)]
 
     for n in range(STEPS):
         for side, no_z, no_y in ((0, slab == 0, tile == 0), (1, slab == SLABS - 1, tile == TILES - 1)):
@@ -190,16 +198,25 @@
                 for z in range(2):
                     zlayers[n][z, side * (CY + 1)] = jnp.zeros((SUB, LANES), jnp.float32)
 
+    def pack_z(n):
+        for side in range(2):
+            sent_z[n, side] = lams[n][side * (CZ - 1)].reshape(CY // 2, 2 * SUB, LANES).astype(jnp.bfloat16)
+
+    def pack_y(n):
+        for side in range(2):
+            sent_y[n, side] = lams[n][:, side * (CY - 1)].reshape(CZ // 2, 2 * SUB, LANES).astype(jnp.bfloat16)
+
     def message(n, d):
         dz, dy = DIRS[d]
-        src_z = {-1: 0, 0: pl.ds(0, CZ), 1: CZ - 1}[dz]
-        src_y = {-1: 0, 0: pl.ds(0, CY), 1: CY - 1}[dy]
-        if dz:
-            dst = zlayers[n].at[int(dz < 0), {-1: CY + 1, 0: pl.ds(1, CY), 1: 0}[dy]]
+        if dy == 0:
+            src, dst = sent_z.at[n, int(dz > 0)], came_z.at[n, int(dz < 0)]
+        elif dz == 0:
+            src, dst = sent_y.at[n, int(dy > 0)], came_y.at[n, int(dy < 0)]
         else:
-            dst = ylayers[n].at[int(dy < 0)]
+            src = lams[n].at[0 if dz < 0 else CZ - 1, 0 if dy < 0 else CY - 1]
+            dst = zlayers[n].at[int(dz < 0), CY + 1 if dy < 0 else 0]
         return pltpu.make_async_remote_copy(
-            src_ref=lams[n].at[src_z, src_y],
+            src_ref=src,
             dst_ref=dst,
             send_sem=send_sem.at[n, d],
             recv_sem=recv_sem.at[n, d],
@@ -219,6 +236,24 @@
             @pl.when(has(-dz, -dy))
             def _():
                 message(n, d).wait_recv()
+                if dy == 0:
+                    side = int(dz < 0)
+                    zlayers[n][side, pl.ds(1, CY)] = (
+                        came_z[n, side].astype(jnp.float32).reshape(CY, SUB, LANES)
+                    )
+                elif dz == 0:
+                    side = int(dy < 0)
+                    ylayers[n][side] = came_y[n, side].astype(jnp.float32).reshape(CZ, SUB, LANES)
+
+    def owner_of(k):
+        return (((tile >> 2) + k // SIDE) & 3) * SIDE + ((tile + k) & 3)
+
+    def ids_to(k):
+        owner = owner_of(k)
+        return pltpu.make_async_remote_copy(
+            src_ref=id_v.at[owner], dst_ref=got_ids.at[k], send_sem=id_send.at[k], recv_sem=id_recv.at[k],
+            device_id=(slab, owner), device_id_type=MESH,
+        )
 
     first = stepper(lam0, zlayers[0], ylayers[0], before, keep, cour, lam1)
     second = stepper(lam1, zlayers[1], ylayers[1], lam0, keep, cour, lam2, cell_s, got1)
@@ -227,93 +262,31 @@
     def outer(n, step):
         receive(n - 1)
         step[1]()
+        pack_z(n)
         send(n, range(6))
         step[2]()
+        pack_y(n)
         send(n, range(6, 8))
 
+    pack_z(0)
+    pack_y(0)
     first[0](1, 5)
-    pl.semaphore_wait(barrier, zs * ys - 1)
+    pl.semaphore_wait(barrier, zs * ys + SLABS + TILES - 2)
     send(0, range(8))
     first[0](6, CZ - 2)
     outer(1, first)
-    pltpu.make_async_copy(cell, cell_s, cell_sem).wait()
+    for load in loads:
+        load.wait()
     second[0](1, CZ - 2)
+    for k in OFFSETS:
+        ids_to(k).start()
     outer(2, second)
-    third[0](1, EARLY)
+    third[0](1, CZ - 2)
     receive(2)
-    for n in range(STEPS):
-        for d in range(8):
-            @pl.when(has(*DIRS[d]))
-            def _():
-                message(n, d).wait_send()
-
-
-def last_kernel(
-    lam1, lam2, begun, begun2, layer_z, layer_y, keep, cour, cell,
-    lam3, final, previous, got2,
-    cell_s, cell_sem, out_sem,
-):
-    del begun, begun2
-
-    def writes(src, dst, first, count, sem):
-        return [
-            pltpu.make_async_copy(
-                src.at[pl.ds(first, count), :, s, :],
-                dst.at[pl.ds(first, count), :, pl.ds(s * LANES, LANES)],
-                out_sem.at[sem, s],
-            )
-            for s in range(SUB)
-        ]
-
-    copies = writes(lam2, previous, 0, CZ, 0)
-    pltpu.make_async_copy(cell, cell_s, cell_sem).start()
-    for copy in copies:
-        copy.start()
-    pltpu.make_async_copy(cell, cell_s, cell_sem).wait()
-    inside, layers, edges = stepper(lam2, layer_z, layer_y, lam1, keep, cour, lam3, cell_s, got2)
-
-    edges()
-    layers()
-    done = 1 + EARLY
-    head = writes(lam3, final, 0, done, 1)
-    for copy in head:
-        copy.start()
-    inside(done, CZ - 2)
-    tail = writes(lam3, final, done, CZ - done, 2)
-    for copy in tail:
-        copy.start()
-    for copy in copies + head + tail:
-        copy.wait()
-
-
-def patch_kernel(
-    cell, count, ids, cells, lam3, got1, got2, history,
-    out,
-    cell_s, count_s, stage, got_rows, got_ids, onehots, got3, total, chunks, result,
-    small_sem, id_send, id_recv, row_send, row_recv, part_send, part_recv, all_send, all_recv,
-):
-    slab, tile = lax.axis_index("slab"), lax.axis_index("tile")
-    barrier = pltpu.get_barrier_semaphore()
-    for k in range(1, TILES):
-        pl.semaphore_signal(barrier, inc=1, device_id=(slab, (tile + k) % TILES), device_id_type=MESH)
-    for k in range(1, SLABS):
-        pl.semaphore_signal(barrier, inc=1, device_id=((slab + k) % SLABS, tile), device_id_type=MESH)
-    small = [(cell, cell_s), (count, count_s)]
-    for i, (src, dst) in enumerate(small):
-        pltpu.make_async_copy(src, dst, small_sem.at[i]).start()
-    for i, (src, dst) in enumerate(small):
-        pltpu.make_async_copy(src, dst, small_sem.at[i]).wait()
+    third[1]()
+    third[2]()
+    flat3 = lam3.reshape(FLAT, LANES)
     shape = (CAP, LANES)
-
-    def owner_of(k):
-        return (((tile >> 2) + k // SIDE) & 3) * SIDE + ((tile + k) & 3)
-
-    def ids_to(k):
-        owner = owner_of(k)
-        return pltpu.make_async_remote_copy(
-            src_ref=ids.at[owner], dst_ref=got_ids.at[k], send_sem=id_send.at[k], recv_sem=id_recv.at[k],
-            device_id=(slab, owner), device_id_type=MESH,
-        )
 
     def rows_to(k, h):
         return pltpu.make_async_remote_copy(
@@ -326,13 +299,13 @@
         j = owner_of(k)
         base = pl.multiple_of(j * CAP, CAP)
         for i in range(CAP):
-            got3[pl.ds(i, 1), :] = lam3[pl.ds(cell_s[base + i] >> 7, 1), :]
-        lane = jnp.broadcast_to((cells[pl.ds(j, 1), :] & 127).astype(jnp.float32), shape).T
+            got3[pl.ds(i, 1), :] = flat3[pl.ds(cell_s[base + i] >> 7, 1), :]
+        lane = jnp.broadcast_to((cell_v[pl.ds(j, 1), :] & 127).astype(jnp.float32), shape).T
         here = lane.astype(jnp.int32) == lax.broadcasted_iota(jnp.int32, shape, 1)
         acc = jnp.zeros((CAP, K), jnp.float32)
         for n, got in enumerate((got1[pl.ds(base, CAP), :], got2[pl.ds(base, CAP), :], got3[...])):
             value = jnp.sum(jnp.where(here, got, 0.0), axis=1, keepdims=True)
-            acc = acc + value * history[n, pl.ds(base, CAP), :].astype(jnp.float32)
+            acc = acc + value * hist[n, pl.ds(base, CAP), :].astype(jnp.float32)
         live = lax.broadcasted_iota(jnp.int32, (CAP, K), 0) < count_s[j]
         acc = jnp.where(live, acc, 0.0).astype(jnp.bfloat16)
         for h in range(HALVES):
@@ -345,14 +318,11 @@
 
     for k in OFFSETS:
         make_rows(k)
-    pl.semaphore_wait(barrier, TILES + SLABS - 2)
+        rows_to(k, 0).start()
     for k in OFFSETS:
-        ids_to(k).start()
-    for h in range(HALVES):
-        for k in OFFSETS:
-            rows_to(k, h).start()
+        rows_to(k, 1).start()
     make_rows(0)
-    onehots[0] = onehot_of(ids[tile])
+    onehots[0] = onehot_of(id_v[tile])
     for h in range(HALVES):
         total[h] = jnp.dot(onehots[0], stage[h, 0], preferred_element_type=jnp.float32)
     for k in OFFSETS:
@@ -392,7 +362,7 @@
         for k in range(1, SLABS):
             to_slab(k, h).wait_recv()
             whole = whole + chunks[h, k]
-        result[h, mine, :] = whole
+        result[h, mine, :] = whole.astype(jnp.bfloat16)
         for k in range(1, SLABS):
             to_all(k, h).start()
 
@@ -406,7 +376,12 @@
     for h in range(HALVES):
         for k in range(1, SLABS):
             to_all(k, h, True).wait_recv()
-        out[:, h * WIDE:(h + 1) * WIDE] = result[h]
+        out[:, h * WIDE:(h + 1) * WIDE] = result[h].astype(jnp.float32)
+    for n in range(STEPS):
+        for d in range(8):
+            @pl.when(has(*DIRS[d]))
+            def _():
+                message(n, d).wait_send()
     for k in OFFSETS:
         ids_to(k).wait_send()
         for h in range(HALVES):
@@ -417,7 +392,19 @@
             to_all(k, h).wait_send()
 
 
-SMEM = pl.BlockSpec(memory_space=pltpu.SMEM)
+def write_kernel(lam2, lam3, result, gradient, final, previous, out_sem, sum_sem):
+    copies = [pltpu.make_async_copy(result, gradient, sum_sem)]
+    for i, (src, dst) in enumerate(((lam2, previous), (lam3, final))):
+        for s in range(SUB):
+            copies.append(
+                pltpu.make_async_copy(src.at[:, :, s, :], dst.at[:, :, pl.ds(s * LANES, LANES)], out_sem.at[i, s])
+            )
+    for copy in copies:
+        copy.start()
+    for copy in copies:
+        copy.wait()
+
+
 VMEM = pl.BlockSpec(memory_space=pltpu.VMEM)
 HBM = pl.BlockSpec(memory_space=pltpu.HBM)
 F32, BF16, I32 = jnp.float32, jnp.bfloat16, jnp.int32
@@ -438,7 +425,7 @@
     picked = pltpu.VMEM((SLOTS, LANES), F32)
     cells = wall_cell.reshape(TILES, CAP)
     damps = wall_damp.reshape(TILES, CAP)
-    cell_s, count_s = pltpu.SMEM((SLOTS,), I32), pltpu.SMEM((TILES,), I32)
+    count_s = pltpu.SMEM((TILES,), I32)
     keep, lam0, before, cour = pl.pallas_call(
         damp_kernel,
         out_shape=(pltpu.VMEM((FLAT, LANES), F32), field, field, field),
@@ -453,55 +440,45 @@
         name="damp",
     )(*in_hbm(block_count, cells, damps, adjoint, adjoint_prev, courant))
     keep = keep.reshape(FIELD)
-    zlayer, ylayer = (2, CY + 2, SUB, LANES), (2, CZ, SUB, LANES)
-    lam1, lam2, begun, layer_z, layer_y, got1, begun2 = pl.pallas_call(
-        steps_kernel,
-        out_shape=(field, field, field, pltpu.VMEM(zlayer, F32), pltpu.VMEM(ylayer, F32), picked, picked),
-        in_specs=[VMEM] * 4 + [HBM],
-        out_specs=(VMEM,) * 7,
+    face_z = pltpu.VMEM((STEPS, 2, CY // 2, 2 * SUB, LANES), BF16)
+    face_y = pltpu.VMEM((STEPS, 2, CZ // 2, 2 * SUB, LANES), BF16)
+    lam2, lam3, result = pl.pallas_call(
+        wave_kernel,
+        out_shape=(field, field, pltpu.VMEM((OWN, K), F32)),
+        in_specs=[VMEM] * 4 + [HBM] * 5,
+        out_specs=(VMEM,) * 3,
         scratch_shapes=[
-            pltpu.VMEM((2, *zlayer), F32), pltpu.VMEM((2, *ylayer), F32), cell_s,
-            DMA, DMA((3, 8)), DMA((3, 8)),
-        ],
-        compiler_params=pltpu.CompilerParams(
-            vmem_limit_bytes=5 * MIB, collective_id=0, has_side_effects=True
-        ),
-        name="steps",
-    )(*in_vmem(lam0, before, cour, keep), *in_hbm(wall_cell))
-    whole = jax.ShapeDtypeStruct((CZ, CY, NX), F32)
-    lam3, final, previous, got2 = pl.pallas_call(
-        last_kernel,
-        out_shape=(field, whole, whole, picked),
-        in_specs=[VMEM] * 8 + [HBM],
-        out_specs=(VMEM, HBM, HBM, VMEM),
-        scratch_shapes=[cell_s, DMA, DMA((3, SUB))],
-        input_output_aliases={2: 0, 3: 3},
-        compiler_params=pltpu.CompilerParams(vmem_limit_bytes=4 * MIB),
-        name="last",
-    )(*in_vmem(lam1, lam2, begun, begun2, layer_z, layer_y, keep, cour), *in_hbm(wall_cell))
-    gradient = pl.pallas_call(
-        patch_kernel,
-        out_shape=jax.ShapeDtypeStruct((OWN, K), F32),
-        in_specs=[HBM, HBM] + [VMEM] * 6,
-        out_specs=VMEM,
-        scratch_shapes=[
-            cell_s, count_s,
+            field, pltpu.VMEM((STEPS, 2, CY + 2, SUB, LANES), F32), pltpu.VMEM((STEPS, 2, CZ, SUB, LANES), F32),
+            face_z, face_y, face_z, face_y,
+            picked, picked, pltpu.VMEM((CAP, LANES), F32),
+            pltpu.SMEM((SLOTS,), I32), count_s, pltpu.VMEM((TILES, CAP), I32), pltpu.VMEM((TILES, 1, CAP), I32),
+            pltpu.VMEM((STEPS, SLOTS, K), BF16),
             pltpu.VMEM((HALVES, TILES, CAP, WIDE), BF16), pltpu.VMEM((HALVES, TILES, CAP, WIDE), BF16),
-            pltpu.VMEM((TILES, 1, CAP), I32), pltpu.VMEM((TILES, OWN, CAP), BF16), pltpu.VMEM((CAP, LANES), F32),
+            pltpu.VMEM((TILES, 1, CAP), I32), pltpu.VMEM((TILES, OWN, CAP), BF16),
             pltpu.VMEM((HALVES, OWN, WIDE), F32), pltpu.VMEM((HALVES, SLABS, PART, WIDE), F32),
-            pltpu.VMEM((HALVES, OWN, WIDE), F32),
-            DMA((2,)), DMA((TILES,)), DMA((TILES,)), DMA((HALVES, TILES)), DMA((HALVES, TILES)),
+            pltpu.VMEM((HALVES, OWN, WIDE), BF16),
+            DMA((5,)), DMA((STEPS, 8)), DMA((STEPS, 8)),
+            DMA((TILES,)), DMA((TILES,)), DMA((HALVES, TILES)), DMA((HALVES, TILES)),
             DMA((HALVES, SLABS)), DMA((HALVES, SLABS)), DMA((HALVES, SLABS)), DMA((HALVES, SLABS)),
         ],
         compiler_params=pltpu.CompilerParams(
-            vmem_limit_bytes=8 * MIB, collective_id=1, has_side_effects=True
+            vmem_limit_bytes=20 * MIB, collective_id=0, has_side_effects=True
         ),
-        name="patch",
+        name="wave",
     )(
-        *in_hbm(wall_cell, block_count),
-        wall_patch.reshape(TILES, 1, CAP), cells,
-        *in_vmem(lam3.reshape(FLAT, LANES), got1, got2), history,
+        *in_vmem(lam0, before, cour, keep),
+        *in_hbm(wall_cell, block_count, cells, wall_patch.reshape(TILES, 1, CAP), history),
     )
+    whole = jax.ShapeDtypeStruct((CZ, CY, NX), F32)
+    gradient, final, previous = pl.pallas_call(
+        write_kernel,
+        out_shape=(jax.ShapeDtypeStruct((OWN, K), F32), whole, whole),
+        in_specs=[VMEM] * 3,
+        out_specs=(HBM,) * 3,
+        scratch_shapes=[DMA((2, SUB)), DMA],
+        compiler_params=pltpu.CompilerParams(vmem_limit_bytes=MIB),
+        name="write",
+    )(*in_vmem(lam2, lam3, result))
     return gradient, final, previous
 
 

time: 65.1 us -> 61.8 us (0.949)
  Pallas kernels: 63.4 us -> 61 us
  local copies, waits for them, and re-layouts: 0.72 us -> 0 us
    pallas_call x3 -> x2, Pallas kernels: 57.5 us -> 55.1 us  [the longest x1 51.6 us: on_device(): pl.pallas_call(wave_kernel, out_shape=(field, field, pltpu.VMEM((OWN, K),...]
    unnamed x5 -> x0, local copies, waits for them, and re-layouts: 0.72 us -> none
where the time goes in v3:
time: 61.8 us; the launch traced here: 61.6 us
  Pallas kernels  61 us (99%)
  between operations  0.65 us (1%)
    pallas_call x1, Pallas kernels, on_device(): pl.pallas_call(wave_kernel, out_shape=(field, field, pltpu.VMEM((OWN, K),...  51.6 us
    pallas_call x1, Pallas kernels, on_device(): pl.pallas_call(damp_kernel, out_shape=(pltpu.VMEM((FLAT, LANES), F32), fi...  5.93 us
    pallas_call x1, Pallas kernels, on_device(): pl.pallas_call(write_kernel, out_shape=(jax.ShapeDtypeStruct((OWN, K), F3...  3.51 us

profile of v3, /device:TPU:1, one launch (start us, length us, event | category | flops | bytes accessed | tf_op | source)
XLA Modules:
  0.0 61.6 jit_solution(3578190278265027630)
XLA Ops:
  0.6 5.9 %damp.1 = (f32[8192,128]{1,0:T(8,128)S(1)}, f32[16,64,8,128]{3,2,1,0:T(8,128)S(1)}, f32[16,64,8,128]{3,2,1,0:T(8,128)S(1)}, f32[16,64,8,128]{3,2,1,0:T(8,128)S(1)}) custom-call(s32[16]{0:T(128)} %count.3, s32[16,128]{1,0:T(8,128)} %bitcast.5, f32[16,128]{1,0:T(8,128)} %bitcast.7, f32[16,64,1024]{2,1,0:T(8,128)} %adjoint.1, f32[16,64,1024]{2,1,0:T(8,128)} %adjoint_prev.1, ...), custom_call_target="tpu_custom_call" | custom-call | tf_op jit(solution)/shard_map/damp/pallas_call | solution.py:429
  6.6 51.6 %wave.1 = (f32[16,64,8,128]{3,2,1,0:T(8,128)S(1)}, f32[16,64,8,128]{3,2,1,0:T(8,128)S(1)}, f32[256,256]{1,0:T(8,128)S(1)}) custom-call(f32[16,64,8,128]{3,2,1,0:T(8,128)S(1)} %get-tuple-element.10.lam0, f32[16,64,8,128]{3,2,1,0:T(8,128)S(1)} %get-tuple-element.11.before, f32[16,64,8,128]{3,2,1,0:T(8,128)S(1)} %get-tuple-element.12.cour, ...), custom_call_target="tpu_custom_call" | custom-call | tf_op jit(solution)/shard_map/wave/pallas_call | solution.py:445
  58.1 3.5 %write.1 = (f32[256,256]{1,0:T(8,128)}, f32[16,64,1024]{2,1,0:T(8,128)}, f32[16,64,1024]{2,1,0:T(8,128)}) custom-call(f32[16,64,8,128]{3,2,1,0:T(8,128)S(1)} %get-tuple-element.14.lam2, f32[16,64,8,128]{3,2,1,0:T(8,128)S(1)} %get-tuple-element.15.lam3, f32[256,256]{1,0:T(8,128)S(1)} %get-tuple-element.16.result), custom_call_target="tpu_custom_call" | custom-call | tf_op jit(solution)/shard_map/write/pallas_call | solution.py:473

commit v4 on v3

--- a/solution.py
+++ b/solution.py
@@ -14,6 +14,7 @@
 CAP = SLOTS // TILES
 OWN = PATCHES // TILES
 HALVES, WIDE = 2, 128
+FAR_SLABS = (4, 3, 5, 2, 6, 1, 7)
 PART = OWN // SLABS
 MESH = pl.DeviceIdType.MESH
 MIB = 1 << 20
@@ -71,7 +72,7 @@
         inc[pl.ds(pl.multiple_of(j * CAP, CAP), CAP), :] = place(high) + place(mid) + place(low)
         return carry
 
-    lax.fori_loop(0, TILES, loss, 0, unroll=4)
+    lax.fori_loop(0, TILES, loss, 0, unroll=8)
     table.wait()
 
     def block(j, carry):
@@ -141,7 +142,7 @@
 
     def layers():
         for z in (0, CZ - 1):
-            rows(z, 0, CY, z)
+            rows(z, 1, CY - 2, z)
 
     def edges():
         def edge(i, carry):
@@ -151,6 +152,9 @@
             return carry
 
         lax.fori_loop(0, (CZ - 2) // 7, edge, 0)
+        for z in (0, CZ - 1):
+            rows(z, 0, 1)
+            rows(z, CY - 1, 1)
 
     return inside, layers, edges
 
@@ -261,12 +265,12 @@
 
     def outer(n, step):
         receive(n - 1)
+        step[2]()
+        pack_y(n)
+        send(n, range(2, 8))
         step[1]()
         pack_z(n)
-        send(n, range(6))
-        step[2]()
-        pack_y(n)
-        send(n, range(6, 8))
+        send(n, range(2))
 
     pack_z(0)
     pack_y(0)
@@ -354,7 +358,7 @@
             total[h] += jnp.dot(onehots[k], got_rows[h, k], preferred_element_type=jnp.float32)
 
     def spread(h):
-        for k in range(1, SLABS):
+        for k in FAR_SLABS:
             to_slab(k, h).start()
 
     def gather(h):
@@ -363,7 +367,7 @@
             to_slab(k, h).wait_recv()
             whole = whole + chunks[h, k]
         result[h, mine, :] = whole.astype(jnp.bfloat16)
-        for k in range(1, SLABS):
+        for k in FAR_SLABS:
             to_all(k, h).start()
 
     add_rows(0, OFFSETS)

time: 61.8 us -> 60.5 us (0.979)
  Pallas kernels: 61 us -> 59.8 us
    pallas_call x1, Pallas kernels: 51.6 us -> 50.6 us  [on_device(): pl.pallas_call(wave_kernel, out_shape=(field, field, pltpu.VMEM((OWN, K),...]
where the time goes in v4:
time: 60.5 us; the launch traced here: 60.4 us
  Pallas kernels  59.8 us (99%)
  between operations  0.65 us (1%)
    pallas_call x1, Pallas kernels, on_device(): pl.pallas_call(wave_kernel, out_shape=(field, field, pltpu.VMEM((OWN, K),...  50.6 us
    pallas_call x1, Pallas kernels, on_device(): pl.pallas_call(damp_kernel, out_shape=(pltpu.VMEM((FLAT, LANES), F32), fi...  5.63 us
    pallas_call x1, Pallas kernels, on_device(): pl.pallas_call(write_kernel, out_shape=(jax.ShapeDtypeStruct((OWN, K), F3...  3.51 us

profile of v4, /device:TPU:1, one launch (start us, length us, event | category | flops | bytes accessed | tf_op | source)
XLA Modules:
  0.0 60.4 jit_solution(7349009227375064880)
XLA Ops:
  0.6 5.6 %damp.1 = (f32[8192,128]{1,0:T(8,128)S(1)}, f32[16,64,8,128]{3,2,1,0:T(8,128)S(1)}, f32[16,64,8,128]{3,2,1,0:T(8,128)S(1)}, f32[16,64,8,128]{3,2,1,0:T(8,128)S(1)}) custom-call(s32[16]{0:T(128)} %count.3, s32[16,128]{1,0:T(8,128)} %bitcast.5, f32[16,128]{1,0:T(8,128)} %bitcast.7, f32[16,64,1024]{2,1,0:T(8,128)} %adjoint.1, f32[16,64,1024]{2,1,0:T(8,128)} %adjoint_prev.1, ...), custom_call_target="tpu_custom_call" | custom-call | tf_op jit(solution)/shard_map/damp/pallas_call | solution.py:433
  6.3 50.6 %wave.1 = (f32[16,64,8,128]{3,2,1,0:T(8,128)S(1)}, f32[16,64,8,128]{3,2,1,0:T(8,128)S(1)}, f32[256,256]{1,0:T(8,128)S(1)}) custom-call(f32[16,64,8,128]{3,2,1,0:T(8,128)S(1)} %get-tuple-element.10.lam0, f32[16,64,8,128]{3,2,1,0:T(8,128)S(1)} %get-tuple-element.11.before, f32[16,64,8,128]{3,2,1,0:T(8,128)S(1)} %get-tuple-element.12.cour, ...), custom_call_target="tpu_custom_call" | custom-call | tf_op jit(solution)/shard_map/wave/pallas_call | solution.py:449
  56.9 3.5 %write.1 = (f32[256,256]{1,0:T(8,128)}, f32[16,64,1024]{2,1,0:T(8,128)}, f32[16,64,1024]{2,1,0:T(8,128)}) custom-call(f32[16,64,8,128]{3,2,1,0:T(8,128)S(1)} %get-tuple-element.14.lam2, f32[16,64,8,128]{3,2,1,0:T(8,128)S(1)} %get-tuple-element.15.lam3, f32[256,256]{1,0:T(8,128)S(1)} %get-tuple-element.16.result), custom_call_target="tpu_custom_call" | custom-call | tf_op jit(solution)/shard_map/write/pallas_call | solution.py:477
